TPU v7x, 256 devices: a whole 4x4x8 slice. The times are simulated.
256 devices in a mesh: dp: 64 (over y, z, core), cand: 4 (over x).
Axes of the slice: x: 4, y: 4, z: 8, core: 2. Of those that a mesh axis runs over, the one named last changes fastest.
Arguments:
- embeddings: bfloat16 [65536, 1024], P('dp')
- point_parent: int32 [65536], P('dp'), may hold values from 0 to 255, as said below
- parent_list: int32 [64, 16], replicated, may hold values from 0 to 255, as said below
- block_slots: int32 [256, 4, 2], replicated, may hold values from 0 to 2047, as said below
- centroids: bfloat16 [2048, 128, 1024], P(('dp', 'cand'))
Outputs:
- new_centroids: bfloat16 [2048, 128, 1024], P(('dp', 'cand'))
- log_partition: float32 [65536], P('dp')
Inputs may be any that keep to these rules, and one draw needn't show every extreme that they name: `point_parent`: the rows of one index of dp belong only to the parents of its entry of parent_list and come in the order of that list; each listed parent has 16 to 112 rows there, and one of them exactly 112. `parent_list`: each index of dp lists 16 distinct parents. `block_slots`: every storage block is named once. Block s lies on the device of index s // 8 of dp+cand (dp slowest), and the blocks of quarter q lie on devices whose cand index is q. The 32 blocks of one quarter that the parents of one index of dp name lie on distinct indices of dp.
All inputs are finite; a program needn't handle non-finite values.
Results may differ from a plain program's by a relative error of at most 0.0065.
Values may be sent and summed in bfloat16 or wider, within the bound.
A program may use at most 192 MiB of HBM per device.

v0:
```python
import jax
import jax.numpy as jnp
from jax import lax
from jax.sharding import PartitionSpec as P

sharpness = 3.0
prior_mass = 1.0


def joined(value, axis, join):
    pieces = jax.tree.map(lambda part: lax.all_gather(part, axis), value)
    head = jax.tree.map(lambda part: part[0], pieces)
    tail = jax.tree.map(lambda part: part[1:], pieces)
    total, _ = lax.scan(lambda total, share: (join(total, share), None), head, tail)
    return total


def combine_parts(former, latter):
    highest = jnp.maximum(former[0], latter[0])
    return (
        highest,
        former[1] * jnp.exp(former[0] - highest) + latter[1] * jnp.exp(latter[0] - highest),
    )


def quarter_total(highest, summed):
    return joined((highest, summed), "cand", combine_parts)


def scaled_logits(scores, blocks):
    squares = jnp.sum(jnp.square(blocks.astype(jnp.float32)), axis=-1)
    return sharpness * (scores - 0.5 * squares[:, None, :])


def finish_update(summed, mass_rows, centroids):
    updated = (summed + prior_mass * centroids.astype(jnp.float32)) / (
        mass_rows[:, :, None] + prior_mass
    )
    return updated.astype(jnp.bfloat16)


def owner_update(got_rows, got_weights, serving, serve_block, centroids):
    stored = centroids.shape[0]
    peer_count = got_rows.shape[0]
    group_size = 8
    rounds = peer_count // group_size
    rows_grouped = got_rows.reshape((rounds, group_size) + got_rows.shape[1:])
    weights_grouped = got_weights.reshape((rounds, group_size) + got_weights.shape[1:])
    blocks_grouped = serve_block.reshape(rounds, group_size)
    serving_grouped = serving.reshape(rounds, group_size)

    def accumulate(running, pieces):
        row_block, weight_block, block_index, is_live = pieces
        partial_value = jnp.einsum(
            "rmn,rmd->rnd", weight_block, row_block, preferred_element_type=jnp.float32
        )
        partial_value = jnp.where(is_live[:, None, None], partial_value, 0.0)
        return (running.at[block_index].add(partial_value), None)

    initial = jnp.zeros((stored,) + centroids.shape[1:], jnp.float32)
    summed, _ = lax.scan(
        accumulate, initial, (rows_grouped, weights_grouped, blocks_grouped, serving_grouped)
    )
    masses = jnp.sum(got_weights.astype(jnp.float32), axis=1)
    masses = jnp.where(serving[:, None], masses, 0.0)
    mass_rows = jnp.zeros(centroids.shape[:2], jnp.float32).at[serve_block].add(masses)
    return finish_update(summed, mass_rows, centroids)


def on_device(embeddings, point_parent, parent_list, block_slots, centroids):
    peer_count = lax.axis_size("dp")
    quarters = lax.axis_size("cand")
    here = lax.axis_index("dp")
    quarter = lax.axis_index("cand")
    row_count = embeddings.shape[0]
    stored = centroids.shape[0]
    listed = parent_list.shape[1]
    halves = block_slots.shape[2]
    mean_rows = row_count // listed
    window = 2 * mean_rows - mean_rows // 4
    listing = jnp.arange(listed, dtype=jnp.int32)
    own_list = parent_list[here]
    position = jnp.sum(
        jnp.where(point_parent[:, None] == own_list[None, :], listing[None, :], 0), axis=1
    )
    starts = jnp.sum((position[None, :] < listing[:, None]).astype(jnp.int32), axis=1)
    starts = jnp.minimum(starts, row_count - window)
    offsets = starts[:, None] + jnp.arange(window, dtype=jnp.int32)[None, :]
    windows = jnp.take(embeddings, offsets, axis=0)
    keep_rows = jnp.take(position, offsets) == listing[:, None]
    quarter_slots = jnp.take(block_slots, quarter, axis=1)
    own_blocks = jnp.take(quarter_slots, own_list, axis=0)
    owner_of = own_blocks // stored // quarters
    peer_ids = jnp.arange(peer_count, dtype=jnp.int32)
    matched = owner_of[None, :, :] == peer_ids[:, None, None]
    needed = jnp.any(matched, axis=(1, 2))
    pick_window = jnp.sum(jnp.where(matched, listing[None, :, None], 0), axis=(1, 2))
    all_blocks = jnp.take(quarter_slots, parent_list, axis=0)
    owned = all_blocks // stored // quarters == here
    serving = jnp.any(owned, axis=(1, 2))
    serve_block = jnp.sum(jnp.where(owned, all_blocks % stored, 0), axis=(1, 2))
    send_rows = jnp.where(needed[:, None, None], jnp.take(windows, pick_window, axis=0), 0)
    got_rows = lax.all_to_all(send_rows, "dp", split_axis=0, concat_axis=0, tiled=True)
    own_part = jnp.take(centroids, serve_block, axis=0)
    scores = jnp.einsum("rmd,rnd->rmn", got_rows, own_part, preferred_element_type=jnp.float32)
    logits = scaled_logits(scores, own_part)
    part_high = jnp.max(logits, axis=2)
    part_sum = jnp.sum(jnp.exp(logits - part_high[:, :, None]), axis=2)
    back_high, back_sum = (
        lax.all_to_all(part_high, "dp", split_axis=0, concat_axis=0, tiled=True),
        lax.all_to_all(part_sum, "dp", split_axis=0, concat_axis=0, tiled=True),
    )
    flat_owner = owner_of.reshape(-1)
    back_high = jnp.take(back_high, flat_owner, axis=0).reshape(listed, halves, window)
    back_sum = jnp.take(back_sum, flat_owner, axis=0).reshape(listed, halves, window)
    highest = back_high[:, 0]
    summed = back_sum[:, 0]
    highest, summed = combine_parts((highest, summed), (back_high[:, 1], back_sum[:, 1]))
    highest, summed = quarter_total(highest, summed)
    log_norm = highest + jnp.log(summed)
    send_norm = jnp.take(log_norm, pick_window, axis=0)
    send_keep = jnp.where(needed[:, None], jnp.take(keep_rows, pick_window, axis=0), False).astype(
        jnp.float32
    )
    got_norm, got_keep = (
        lax.all_to_all(send_norm, "dp", split_axis=0, concat_axis=0, tiled=True),
        lax.all_to_all(send_keep, "dp", split_axis=0, concat_axis=0, tiled=True),
    )
    got_weights = jnp.where(
        got_keep[:, :, None] > 0.5, jnp.exp(logits - got_norm[:, :, None]), 0.0
    ).astype(jnp.bfloat16)
    updated = owner_update(got_rows, got_weights, serving, serve_block, centroids)
    log_partition = log_norm[position, jnp.arange(row_count, dtype=jnp.int32) - starts[position]]
    return (updated, log_partition)


def solution(mesh):
    return jax.shard_map(
        on_device,
        mesh=mesh,
        in_specs=(P("dp", None), P("dp"), P(), P(), P(("dp", "cand"), None, None)),
        out_specs=(P(("dp", "cand"), None, None), P("dp")),
        check_vma=False,
    )
```

profile of v0, /device:TPU:1, one launch (start us, length us, event | category | flops | bytes accessed | tf_op | source)
XLA Modules:
  0.0 605.0 jit_solution(17888512763476579539)
XLA Ops:
  4.6 1.3 select_reduce_fusion
  5.9 1.3 fusion.15
  7.3 2.8 gather_fusion
  11.0 1.6 fusion.14
  13.0 6.7 %gather_fusion.2 = s32[1792]{0:T(1024)S(1)} fusion(s32[1024]{0:T(1024)S(1)} %select_reduce_fusion.1, s32[2048]{0:T(1024)S(1)} %pad_clamp_fusion), kind=kCustom, calls=%fused_computation.4 | custom fusion | bytes 21504 | tf_op jit(solution)/shard_map/jit(_take)/gather | solution.py:90
  19.9 6.6 %gather_fusion.4 = bf16[1792,1024]{1,0:T(8,128)(2,1)} fusion(bf16[1024,1024]{1,0:T(8,128)(2,1)S(1)} %copy-done, s32[2048]{0:T(1024)S(1)} %pad_clamp_fusion), kind=kCustom, calls=%fused_computation.6 | custom fusion | bytes 7347200 | tf_op jit(solution)/shard_map/jit(_take)/gather | solution.py:89
  26.6 3.5 broadcast_select_fusion.2
  30.1 9.9 %gather_fusion.5 = bf16[64,112,1024]{2,1,0:T(8,128)(2,1)} fusion(bf16[16,112,1024]{2,1,0:T(8,128)(2,1)} %broadcast_select_fusion.2, s32[1024]{0:T(1024)S(1)} %pad_clamp_fusion.3), kind=kCustom, calls=%fused_computation.7 | custom fusion | bytes 29360384 | tf_op jit(solution)/shard_map/jit(_take)/gather | solution.py:102
  40.0 13.8 %select_select_fusion = bf16[64,112,1024]{2,1,0:T(8,128)(2,1)} fusion(bf16[64,112,1024]{2,1,0:T(8,128)(2,1)} %gather_fusion.5, pred[64]{0:T(512)(128)(4,1)S(1)} %compare_and_fusion.3, pred[64]{0:T(512)(128)(4,1)S(1)} %fusion.15), kind=kLoop, calls=%fused_computation.31 | loop fusion | flops 14680064 | bytes 29360256 | tf_op jit(solution)/shard_map/jit(_where)/select_n | solution.py:102
  53.8 13.5 %all-to-all-start.1 = ((bf16[64,112,1024]{2,1,0:T(8,128)(2,1)}), bf16[64,112,1024]{2,1,0:T(8,128)(2,1)}, u32[]{:S(2)}, u32[]{:S(2)}) async-start(bf16[64,112,1024]{2,1,0:T(8,128)(2,1)} %select_select_fusion), calls=%async_computation.1 | async-start | bytes 29360128 | tf_op jit(solution)/shard_map/all_to_all | solution.py:103
  68.1 1.3 reduce_or.18
  69.5 7.4 %gather_fusion.6 = bf16[64,128,1024]{2,1,0:T(8,128)(2,1)} fusion(bf16[8,128,1024]{2,1,0:T(8,128)(2,1)S(1)} %copy-done.2, s32[1024]{0:T(1024)S(1)} %pad_clamp_fusion.2), kind=kCustom, calls=%fused_computation.8 | custom fusion | bytes 33554688 | tf_op jit(solution)/shard_map/jit(_take)/gather | solution.py:104
  77.6 4.3 compare_select_fusion.6
  82.1 5.6 select_select_fusion.1
  88.4 7.8 %multiply_reduce_fusion = f32[64,128]{1,0:T(8,128)S(1)} fusion(bf16[64,128,1024]{2,1,0:T(8,128)(2,1)} %gather_fusion.6, pred[64]{0:T(512)(128)(4,1)S(1)} %compare_and_fusion.2), kind=kLoop, calls=%fused_computation.29 | loop fusion | flops 33546240 | bytes 16810048 | tf_op jit(solution)/shard_map/reduce_sum | solution.py:31
  96.3 291.6 %all-to-all-done.1 = bf16[64,112,1024]{2,1,0:T(8,128)(2,1)} async-done(((bf16[64,112,1024]{2,1,0:T(8,128)(2,1)}), bf16[64,112,1024]{2,1,0:T(8,128)(2,1)}, u32[]{:S(2)}, u32[]{:S(2)}) %all-to-all-start.1) | async-done | bytes 14680096 | tf_op jit(solution)/shard_map/all_to_all | solution.py:103
  387.9 14.9 %fusion.10 = (f32[64,112]{1,0:T(8,128)}, f32[64,112,128]{2,1,0:T(8,128)}) fusion(f32[64,128]{1,0:T(8,128)S(1)} %broadcast_multiply_fusion, bf16[64,112,1024]{2,1,0:T(8,128)(2,1)} %all-to-all-done.1, bf16[64,128,1024]{2,1,0:T(8,128)(2,1)} %gather_fusion.6, pred[64]{0:T(512)(128)(4,1)S(1)} %compare_and_fusion.2), kind=kOutput, calls=%fused_computation.39 | convolution fusion | flops 1890182144 | bytes 35188800 | tf_op jit(solution)/shard_map/rmd,rnd->rmn/dot_general | solution.py:105
  402.8 5.9 all-to-all-start.2
  408.8 4.4 exponential_reduce_fusion
  413.1 4.9 all-to-all-done.2
  418.0 5.5 all-to-all-start.3
  424.0 8.7 %all-to-all-done.3 = f32[64,1,112]{2,1,0:T(1,128)S(1)} async-done(((f32[64,1,112]{2,1,0:T(1,128)}), f32[64,1,112]{2,1,0:T(1,128)S(1)}, u32[]{:S(2)}, u32[]{:S(2)}) %all-to-all-start.3) | async-done | bytes 28704 | tf_op jit(solution)/shard_map/all_to_all | solution.py:111
  432.7 4.7 all-to-all-start
  438.2 9.3 %all_gather.9 = f32[4,16,112]{2,1,0:T(8,128)S(1)} all-gather(f32[1,16,112]{2,1,0:T(8,128)S(1)} %get-tuple-element.118), channel_id=1, replica_groups=mesh['dp'=64,'cand'=4] {'cand'}, dimensions={0}, use_global_device_ids=true | all-gather | bytes 35840 | tf_op jit(solution)/shard_map/all_gather | solution.py:11
  447.5 9.0 %all_gather.8 = f32[4,16,112]{2,1,0:T(8,128)S(1)} all-gather(f32[1,16,112]{2,1,0:T(8,128)S(1)} %get-tuple-element.119), channel_id=1, replica_groups=mesh['dp'=64,'cand'=4] {'cand'}, dimensions={0}, use_global_device_ids=true | all-gather | bytes 35840 | tf_op jit(solution)/shard_map/all_gather | solution.py:11
  457.9 16.2 %all-to-all-start.4 = ((f32[64,1,112]{2,1,0:T(1,128)}), f32[64,1,112]{2,1,0:T(1,128)S(1)}, u32[]{:S(2)}, u32[]{:S(2)}) async-start(f32[64,1,112]{2,1,0:T(1,128)} %bitcast.32), calls=%async_computation.4 | async-start | bytes 65536 | tf_op jit(solution)/shard_map/all_to_all | solution.py:126
  474.2 11.2 %gather_fusion.8 = f32[1024]{0:T(1024)} fusion(f32[16,112]{1,0:T(8,128)S(1)} %log_add_fusion, s32[1024]{0:T(1024)S(1)} %bitcast.145), kind=kCustom, calls=%fused_computation.10 | custom fusion | bytes 16384 | tf_op jit(solution)/shard_map/gather | solution.py:133
  485.4 5.8 convert_reduce_fusion
  491.2 2.5 broadcast_in_dim.215
  493.7 105.1 %while.24 = (s32[]{:T(128)}, f32[8,128,1024]{2,1,0:T(8,128)}, s32[8,8]{1,0:T(8,128)S(1)}, pred[8,8]{1,0:T(8,128)(4,1)S(1)}, bf16[8,8,112,128]{3,2,1,0:T(8,128)(2...) while((s32[]{:T(128)}, f32[8,128,1024]{2,1,0:T(8,128)}, s32[8,8]{1,0:T(8,128)S(1)}, ...), condition=%wide.region_13.15_spmd, body=%wide.region_11.14_spmd.sunk | while | flops 236978208 | bytes 18843332 | solution.py:61
  493.7 4.2 convolution_select_fusion.2
  497.9 8.7 %scatter_fusion = f32[8,128,1024]{2,1,0:T(8,128)} fusion(f32[8,128,1024]{2,1,0:T(8,128)} %get-tuple-element.246, s32[8]{0:T(128)S(1)} %fusion.54, f32[8,128,1024]{2,1,0:T(8,128)} %convolution_select_fusion.2), kind=kCustom, calls=%fused_computation.11.clone.1 | custom fusion | flops 1048576 | bytes 12582944 | tf_op jit(solution)/shard_map/while/body/eval_jaxpr/scatter-add | solution.py:58
  506.7 4.2 convolution_select_fusion.2
  510.9 8.9 %scatter_fusion = f32[8,128,1024]{2,1,0:T(8,128)} fusion(f32[8,128,1024]{2,1,0:T(8,128)} %get-tuple-element.246, s32[8]{0:T(128)S(1)} %fusion.54, f32[8,128,1024]{2,1,0:T(8,128)} %convolution_select_fusion.2), kind=kCustom, calls=%fused_computation.11.clone.1 | custom fusion | flops 1048576 | bytes 12582944 | tf_op jit(solution)/shard_map/while/body/eval_jaxpr/scatter-add | solution.py:58
  519.8 4.2 convolution_select_fusion.2
  524.1 8.9 %scatter_fusion = f32[8,128,1024]{2,1,0:T(8,128)} fusion(f32[8,128,1024]{2,1,0:T(8,128)} %get-tuple-element.246, s32[8]{0:T(128)S(1)} %fusion.54, f32[8,128,1024]{2,1,0:T(8,128)} %convolution_select_fusion.2), kind=kCustom, calls=%fused_computation.11.clone.1 | custom fusion | flops 1048576 | bytes 12582944 | tf_op jit(solution)/shard_map/while/body/eval_jaxpr/scatter-add | solution.py:58
  533.0 4.2 convolution_select_fusion.2
  537.2 8.7 %scatter_fusion = f32[8,128,1024]{2,1,0:T(8,128)} fusion(f32[8,128,1024]{2,1,0:T(8,128)} %get-tuple-element.246, s32[8]{0:T(128)S(1)} %fusion.54, f32[8,128,1024]{2,1,0:T(8,128)} %convolution_select_fusion.2), kind=kCustom, calls=%fused_computation.11.clone.1 | custom fusion | flops 1048576 | bytes 12582944 | tf_op jit(solution)/shard_map/while/body/eval_jaxpr/scatter-add | solution.py:58
  546.0 4.2 convolution_select_fusion.2
  550.2 8.9 %scatter_fusion = f32[8,128,1024]{2,1,0:T(8,128)} fusion(f32[8,128,1024]{2,1,0:T(8,128)} %get-tuple-element.246, s32[8]{0:T(128)S(1)} %fusion.54, f32[8,128,1024]{2,1,0:T(8,128)} %convolution_select_fusion.2), kind=kCustom, calls=%fused_computation.11.clone.1 | custom fusion | flops 1048576 | bytes 12582944 | tf_op jit(solution)/shard_map/while/body/eval_jaxpr/scatter-add | solution.py:58
  559.1 4.2 convolution_select_fusion.2
  563.4 8.9 %scatter_fusion = f32[8,128,1024]{2,1,0:T(8,128)} fusion(f32[8,128,1024]{2,1,0:T(8,128)} %get-tuple-element.246, s32[8]{0:T(128)S(1)} %fusion.54, f32[8,128,1024]{2,1,0:T(8,128)} %convolution_select_fusion.2), kind=kCustom, calls=%fused_computation.11.clone.1 | custom fusion | flops 1048576 | bytes 12582944 | tf_op jit(solution)/shard_map/while/body/eval_jaxpr/scatter-add | solution.py:58
  572.3 4.2 convolution_select_fusion.2
  576.5 8.9 %scatter_fusion = f32[8,128,1024]{2,1,0:T(8,128)} fusion(f32[8,128,1024]{2,1,0:T(8,128)} %get-tuple-element.246, s32[8]{0:T(128)S(1)} %fusion.54, f32[8,128,1024]{2,1,0:T(8,128)} %convolution_select_fusion.2), kind=kCustom, calls=%fused_computation.11.clone.1 | custom fusion | flops 1048576 | bytes 12582944 | tf_op jit(solution)/shard_map/while/body/eval_jaxpr/scatter-add | solution.py:58
  585.4 4.2 convolution_select_fusion.2
  589.7 9.1 %scatter_fusion = f32[8,128,1024]{2,1,0:T(8,128)} fusion(f32[8,128,1024]{2,1,0:T(8,128)} %get-tuple-element.246, s32[8]{0:T(128)S(1)} %fusion.54, f32[8,128,1024]{2,1,0:T(8,128)} %convolution_select_fusion.2), kind=kCustom, calls=%fused_computation.11.clone.1 | custom fusion | flops 1048576 | bytes 12582944 | tf_op jit(solution)/shard_map/while/body/eval_jaxpr/scatter-add | solution.py:58
  598.8 1.0 scatter_custom_fusion.1
  599.8 5.2 divide_convert_fusion
  (84 shorter events, 10.9 us)
Async XLA Ops:
  0.6 19.3 %copy-start = (bf16[1024,1024]{1,0:T(8,128)(2,1)S(1)}, bf16[1024,1024]{1,0:T(8,128)(2,1)}, u32[]{:S(2)}) copy-start(bf16[1024,1024]{1,0:T(8,128)(2,1)} %param.11) | copy-start | bytes 6291460
  0.6 12.0 %copy-start.3 = (s32[1024]{0:T(1024)S(1)}, s32[1024]{0:T(1024)}, u32[]{:S(2)}) copy-start(s32[1024]{0:T(1024)} %param.12) | copy-start | bytes 12292
  53.8 15.7 %copy-start.2 = (bf16[8,128,1024]{2,1,0:T(8,128)(2,1)S(1)}, bf16[8,128,1024]{2,1,0:T(8,128)(2,1)}, u32[]{:S(2)}) copy-start(bf16[8,128,1024]{2,1,0:T(8,128)(2,1)} %param.15) | copy-start | bytes 6291460
  53.8 334.1 %all-to-all-start.1 = ((bf16[64,112,1024]{2,1,0:T(8,128)(2,1)}), bf16[64,112,1024]{2,1,0:T(8,128)(2,1)}, u32[]{:S(2)}, u32[]{:S(2)}) async-start(bf16[64,112,1024]{2,1,0:T(8,128)(2,1)} %select_select_fusion), calls=%async_computation.1 | async-start | bytes 29360128 | tf_op jit(solution)/shard_map/all_to_all | solution.py:103
  402.8 15.2 %all-to-all-start.2 = ((f32[64,1,112]{2,1,0:T(1,128)}), f32[64,1,112]{2,1,0:T(1,128)S(1)}, u32[]{:S(2)}, u32[]{:S(2)}) async-start(f32[64,1,112]{2,1,0:T(1,128)} %bitcast.19), calls=%async_computation.2 | async-start | bytes 65536 | tf_op jit(solution)/shard_map/all_to_all | solution.py:110
  418.0 14.8 %all-to-all-start.3 = ((f32[64,1,112]{2,1,0:T(1,128)}), f32[64,1,112]{2,1,0:T(1,128)S(1)}, u32[]{:S(2)}, u32[]{:S(2)}) async-start(f32[64,1,112]{2,1,0:T(1,128)} %bitcast.25), calls=%async_computation.3 | async-start | bytes 65536 | tf_op jit(solution)/shard_map/all_to_all | solution.py:111
  432.7 25.2 %all-to-all-start = ((f32[64,1,112]{2,1,0:T(1,128)}), f32[64,1,112]{2,1,0:T(1,128)S(1)}, u32[]{:S(2)}, u32[]{:S(2)}) async-start(f32[64,1,112]{2,1,0:T(1,128)} %bitcast.13), calls=%async_computation | async-start | bytes 65536 | tf_op jit(solution)/shard_map/all_to_all | solution.py:127
  457.9 27.5 %all-to-all-start.4 = ((f32[64,1,112]{2,1,0:T(1,128)}), f32[64,1,112]{2,1,0:T(1,128)S(1)}, u32[]{:S(2)}, u32[]{:S(2)}) async-start(f32[64,1,112]{2,1,0:T(1,128)} %bitcast.32), calls=%async_computation.4 | async-start | bytes 65536 | tf_op jit(solution)/shard_map/all_to_all | solution.py:126
  599.8 5.2 copy-start.1
where the time goes:
time: 607 us; the launch traced here: 605 us
  waiting for transfers between devices  305 us (50%)
  other arithmetic  133 us (22%)
  local copies, waits for them, and re-layouts  53.3 us (9%)
  matrix products  48.8 us (8%)
  starting transfers between devices  45.8 us (8%)
  blocking collectives  18.4 us (3%)
    all_to_all x1, waiting for transfers between devices, on_device(): lax.all_to_all(send_rows, 'dp', split_axis=0, concat_axis=0, tiled=True)  292 us
    scatter-add x8, other arithmetic, accumulate(): return (running.at[block_index].add(partial_value), None)  71.1 us
    dot_general x8, matrix products, accumulate(): jnp.einsum('rmn,rmd->rnd', weight_block, row_block, preferred_element_typ...  33.9 us
    all_gather x2, blocking collectives, joined(): pieces = jax.tree.map(lambda part: lax.all_gather(part, axis), value)  18.4 us
    all_to_all x1, starting transfers between devices, on_device(): lax.all_to_all(send_norm, 'dp', split_axis=0, concat_axis=0, tiled=True)  16.2 us
    dot_general x1, matrix products, on_device(): jnp.einsum('rmd,rnd->rmn', got_rows, own_part, preferred_element_type=jnp...  14.9 us
    select_n x1, other arithmetic, on_device(): jnp.where(needed[:, None, None], jnp.take(windows, pick_window, axis=0), 0)  13.8 us
    all_to_all x1, starting transfers between devices, on_device(): lax.all_to_all(send_rows, 'dp', split_axis=0, concat_axis=0, tiled=True)  13.5 us
  transfers between devices with their start and end apart: 5, of which 3 were waited for; matrix products, arithmetic and copies ran while one was open for 8% of the time, Pallas kernels for 0%

commit v1 on v0

v1 whole, which is shorter than its diff:
```python
import functools

import jax
import jax.numpy as jnp
from jax import lax
from jax.experimental import pallas as pl
from jax.experimental.pallas import tpu as pltpu
from jax.sharding import Mesh
from jax.sharding import PartitionSpec as P

sharpness = 3.0
prior_mass = 1.0

GRAIN = 16
SPAN = 8
NY, NZ, NC, NQ = 4, 8, 2, 4
NDP = NY * NZ * NC
PER_Y = NZ * NC
MESH = pl.DeviceIdType.MESH
VMEM_LIMIT = 56 * 2**20


def pack_kernel(count, pick_ref, grains_ref, out_ref):
    target = pl.program_id(0)

    @pl.loop(0, count)
    def _(place):
        out_ref[0, place] = grains_ref[pick_ref[target * count + place]]


def pack(grains, picks):
    targets, count = picks.shape
    shape = grains.shape[1:]
    return pl.pallas_call(
        functools.partial(pack_kernel, count),
        grid_spec=pltpu.PrefetchScalarGridSpec(
            num_scalar_prefetch=1,
            grid=(targets,),
            in_specs=[pl.BlockSpec(grains.shape, lambda t, *_: (0, 0, 0))],
            out_specs=pl.BlockSpec((1, count) + shape, lambda t, *_: (t, 0, 0, 0)),
        ),
        out_shape=jax.ShapeDtypeStruct((targets, count) + shape, grains.dtype),
        compiler_params=pltpu.CompilerParams(vmem_limit_bytes=VMEM_LIMIT),
        cost_estimate=pl.CostEstimate(
            flops=0, bytes_accessed=2 * (grains.size + targets * count * shape[0] * shape[1]), transcendentals=0
        ),
    )(picks.reshape(-1), grains)


def window_rows(rows_ref, spot_ref, window):
    parts = [rows_ref[0, spot_ref[window * SPAN + k]] for k in range(SPAN)]
    return jnp.concatenate(parts, axis=0)


def score_kernel(spot_ref, block_ref, low_ref, high_ref, rows_ref, cent_ref, logit_ref, part_ref, square_ref):
    group = pl.program_id(0)

    @pl.when(group == 0)
    def _():
        @pl.loop(0, cent_ref.shape[0])
        def _(b):
            wide = cent_ref[b].astype(jnp.float32)
            square_ref[b] = jnp.sum(wide * wide, axis=1, keepdims=True)

    @pl.loop(0, PER_Y)
    def _(i):
        window = group * PER_Y + i

        @pl.when(high_ref[window] > low_ref[window])
        def _():
            rows = window_rows(rows_ref, spot_ref, window)
            b = block_ref[window]
            scores = lax.dot_general(
                cent_ref[b], rows, (((1,), (1,)), ((), ())), preferred_element_type=jnp.float32
            )
            logits = sharpness * (scores - 0.5 * square_ref[b])
            highest = jnp.max(logits, axis=0, keepdims=True)
            total = jnp.sum(jnp.exp(logits - highest), axis=0, keepdims=True)
            logit_ref[i] = logits
            part_ref[i] = jnp.concatenate([highest, total], axis=0)

        @pl.when(high_ref[window] <= low_ref[window])
        def _():
            part_ref[i] = jnp.zeros(part_ref.shape[1:], jnp.float32)


def update_kernel(spot_ref, block_ref, low_ref, high_ref, rows_ref, cent_ref, logit_ref, norm_ref, out_ref, sum_ref, mass_ref):
    group = pl.program_id(0)

    @pl.when(group == 0)
    def _():
        sum_ref[...] = jnp.zeros_like(sum_ref)
        mass_ref[...] = jnp.zeros_like(mass_ref)

    @pl.loop(0, PER_Y)
    def _(i):
        window = group * PER_Y + i
        low, high = low_ref[window], high_ref[window]

        @pl.when(high > low)
        def _():
            rows = window_rows(rows_ref, spot_ref, window)
            b = block_ref[window]
            place = lax.broadcasted_iota(jnp.int32, logit_ref.shape[1:], 1)
            keep = (place >= low) & (place < high)
            weights = jnp.where(keep, jnp.exp(logit_ref[i] - norm_ref[i]), 0.0).astype(jnp.bfloat16)
            sum_ref[b] += lax.dot_general(
                weights, rows, (((1,), (0,)), ((), ())), preferred_element_type=jnp.float32
            )
            mass_ref[b] += jnp.sum(weights.astype(jnp.float32), axis=1, keepdims=True)

    @pl.when(group == NY - 1)
    def _():
        @pl.loop(0, cent_ref.shape[0])
        def _(b):
            new = (sum_ref[b] + prior_mass * cent_ref[b].astype(jnp.float32)) / (mass_ref[b] + prior_mass)
            out_ref[b] = new.astype(out_ref.dtype)


def score(rows, spots, block, low, high, centroids):
    stored, lanes, width = centroids.shape
    span = SPAN * GRAIN
    return pl.pallas_call(
        score_kernel,
        grid_spec=pltpu.PrefetchScalarGridSpec(
            num_scalar_prefetch=4,
            grid=(NY,),
            in_specs=[
                pl.BlockSpec((1,) + rows.shape[1:], lambda g, *_: (g, 0, 0, 0)),
                pl.BlockSpec(centroids.shape, lambda g, *_: (0, 0, 0)),
            ],
            out_specs=[
                pl.BlockSpec((PER_Y, lanes, span), lambda g, *_: (g, 0, 0)),
                pl.BlockSpec((PER_Y, 2, span), lambda g, *_: (g, 0, 0)),
            ],
            scratch_shapes=[pltpu.VMEM((stored, lanes, 1), jnp.float32)],
        ),
        out_shape=[
            jax.ShapeDtypeStruct((NDP, lanes, span), jnp.float32),
            jax.ShapeDtypeStruct((NDP, 2, span), jnp.float32),
        ],
        compiler_params=pltpu.CompilerParams(vmem_limit_bytes=VMEM_LIMIT),
        cost_estimate=pl.CostEstimate(
            flops=NDP * lanes * span * width, bytes_accessed=2 * rows.size, transcendentals=NDP * lanes * span
        ),
    )(spots.reshape(-1), block, low, high, rows, centroids)


def update(rows, spots, block, low, high, centroids, logits, norms):
    stored, lanes, width = centroids.shape
    span = SPAN * GRAIN
    return pl.pallas_call(
        update_kernel,
        grid_spec=pltpu.PrefetchScalarGridSpec(
            num_scalar_prefetch=4,
            grid=(NY,),
            in_specs=[
                pl.BlockSpec((1,) + rows.shape[1:], lambda g, *_: (g, 0, 0, 0)),
                pl.BlockSpec(centroids.shape, lambda g, *_: (0, 0, 0)),
                pl.BlockSpec((PER_Y, lanes, span), lambda g, *_: (g, 0, 0)),
                pl.BlockSpec((PER_Y, 1, span), lambda g, *_: (g, 0, 0)),
            ],
            out_specs=pl.BlockSpec(centroids.shape, lambda g, *_: (0, 0, 0)),
            scratch_shapes=[
                pltpu.VMEM((stored, lanes, width), jnp.float32),
                pltpu.VMEM((stored, lanes, 1), jnp.float32),
            ],
        ),
        out_shape=jax.ShapeDtypeStruct(centroids.shape, centroids.dtype),
        compiler_params=pltpu.CompilerParams(vmem_limit_bytes=VMEM_LIMIT),
        cost_estimate=pl.CostEstimate(
            flops=NDP * lanes * span * width, bytes_accessed=2 * rows.size, transcendentals=NDP * lanes * span
        ),
    )(spots.reshape(-1), block, low, high, rows, centroids, logits, norms)


def joint(former, latter):
    highest = jnp.maximum(former[0:1], latter[0:1])
    total = former[1:2] * jnp.exp(former[0:1] - highest) + latter[1:2] * jnp.exp(latter[0:1] - highest)
    return jnp.concatenate([highest, total], axis=0)


def exchange_kernel(
    first_ref, second_ref, pick_ref, part_ref, got_ref, own_ref,
    back_ref, half_ref, quarters_ref, send_ref, land_ref,
    back_send, back_recv, cross_send, cross_recv, fore_send, fore_recv,
):
    y, z, c, q = (lax.axis_index(a) for a in ("y", "z", "core", "cand"))
    here = (y * NZ + z) * NC + c
    listed = own_ref.shape[0]

    def device(index):
        return (index // PER_Y, (index // NC) % NZ, index % NC, q)

    def crossing(step):
        return (y, z, c, (q + step) % NQ)

    barrier = pltpu.get_barrier_semaphore()

    @pl.loop(1, NDP)
    def _(t):
        pl.semaphore_signal(barrier, 1, device_id=device((here + t) % NDP), device_id_type=MESH)

    for step in range(1, NQ):
        pl.semaphore_signal(barrier, 1, device_id=crossing(step), device_id_type=MESH)
    pl.semaphore_wait(barrier, NDP - 1 + NQ - 1)

    def back(t):
        peer = (here + t) % NDP
        return pltpu.make_async_remote_copy(
            part_ref.at[peer], back_ref.at[here], back_send.at[t], back_recv.at[t],
            device_id=device(peer), device_id_type=MESH,
        )

    def fore(t):
        peer = (here + t) % NDP
        return pltpu.make_async_remote_copy(
            send_ref.at[peer], land_ref.at[here], fore_send.at[t], fore_recv.at[t],
            device_id=device(peer), device_id_type=MESH,
        )

    def cross(step):
        return pltpu.make_async_remote_copy(
            half_ref, quarters_ref.at[step], cross_send.at[step], cross_recv.at[step],
            device_id=crossing(step), device_id_type=MESH,
        )

    @pl.loop(1, NDP)
    def _(t):
        back(t).start()

    back_ref[here] = part_ref[here]

    @pl.loop(1, NDP)
    def _(t):
        back(t).wait()

    @pl.loop(0, listed)
    def _(e):
        half_ref[e] = joint(back_ref[first_ref[e]], back_ref[second_ref[e]])

    for step in range(1, NQ):
        cross(step).start()
    for step in range(1, NQ):
        cross(step).wait()

    @pl.loop(0, listed)
    def _(e):
        both = joint(half_ref[e], quarters_ref[1, e])
        rest = joint(quarters_ref[2, e], quarters_ref[3, e])
        pair = joint(both, rest)
        own_ref[e] = pair[0:1] + jnp.log(pair[1:2])

    @pl.loop(0, NDP)
    def _(j):
        send_ref[j] = own_ref[pick_ref[j]]

    @pl.loop(1, NDP)
    def _(t):
        fore(t).start()

    land_ref[here] = send_ref[here]

    @pl.loop(1, NDP)
    def _(t):
        fore(t).wait()

    got_ref[...] = land_ref[...]


def exchange(first, second, pick, part, collective_id):
    listed = first.shape[0]
    span = SPAN * GRAIN
    smem, vmem = pl.BlockSpec(memory_space=pltpu.SMEM), pl.BlockSpec(memory_space=pltpu.VMEM)
    dma = pltpu.SemaphoreType.DMA
    return pl.pallas_call(
        exchange_kernel,
        in_specs=[smem, smem, smem, vmem],
        out_specs=[vmem, vmem],
        out_shape=[
            jax.ShapeDtypeStruct((NDP, 1, span), jnp.float32),
            jax.ShapeDtypeStruct((listed, 1, span), jnp.float32),
        ],
        scratch_shapes=[
            pltpu.VMEM((NDP, 2, span), jnp.float32),
            pltpu.VMEM((listed, 2, span), jnp.float32),
            pltpu.VMEM((NQ, listed, 2, span), jnp.float32),
            pltpu.VMEM((NDP, 1, span), jnp.float32),
            pltpu.VMEM((NDP, 1, span), jnp.float32),
            dma((NDP,)), dma((NDP,)), dma((NQ,)), dma((NQ,)), dma((NDP,)), dma((NDP,)),
        ],
        compiler_params=pltpu.CompilerParams(
            collective_id=collective_id, has_side_effects=True, vmem_limit_bytes=16 * 2**20
        ),
    )(first, second, pick, part)


def on_device(embeddings, point_parent, parent_list, block_slots, centroids):
    y, z, c, q = (lax.axis_index(a) for a in ("y", "z", "core", "cand"))
    here = (y * NZ + z) * NC + c
    row_count, width = embeddings.shape
    stored = centroids.shape[0]
    listed = parent_list.shape[1]
    grains = row_count // GRAIN
    local = grains // NQ
    i32 = jnp.int32

    share = lax.dynamic_index_in_dim(embeddings.reshape(local, NQ, GRAIN, width), q, 1, keepdims=False)
    shares = lax.all_gather(share, "z", axis=0, tiled=True)

    counts = jnp.sum((point_parent[:, None] == parent_list[here][None, :]).astype(i32), axis=0)
    counts = lax.all_gather(counts, ("y", "z", "core"), axis=0)
    starts = jnp.cumsum(counts, axis=1) - counts
    grain0 = starts // GRAIN
    low = starts % GRAIN
    high = low + counts
    slots = jnp.take(block_slots, parent_list, axis=0)
    owner = slots // (stored * NQ)

    mine = jnp.take(owner, q, axis=2) == here
    entry = jnp.any(mine, axis=2)
    chosen = lambda value: jnp.sum(jnp.where(entry, value, 0), axis=1)
    serve_low, serve_high, serve_grain = chosen(low), chosen(high), chosen(grain0)
    serve_block = jnp.sum(jnp.where(mine, jnp.take(slots, q, axis=2) % stored, 0), axis=(1, 2))

    dps = jnp.arange(NDP, dtype=i32)
    own_owner = lax.dynamic_index_in_dim(jnp.take(owner, q, axis=2), here, 0, keepdims=False)
    pick = jnp.sum(
        jnp.where(own_owner[None] == dps[:, None, None], jnp.arange(listed, dtype=i32)[None, :, None], 0), axis=(1, 2)
    )

    def by_place(value):
        return value.reshape((NY, NZ, NC) + value.shape[1:])

    src_owner = lax.dynamic_index_in_dim(by_place(owner), y, 0, keepdims=False)
    src_owner = lax.dynamic_index_in_dim(src_owner, c, 1, keepdims=False)
    src_grain = lax.dynamic_index_in_dim(by_place(grain0), y, 0, keepdims=False)
    src_grain = lax.dynamic_index_in_dim(src_grain, c, 1, keepdims=False)
    target = (jnp.arange(NY, dtype=i32)[:, None] * NZ + z) * NC + jnp.arange(NC, dtype=i32)[None, :]
    hit = jnp.any(src_owner[None, None] == target[:, :, None, None, None, None], axis=-1)
    begin = jnp.sum(jnp.where(hit, src_grain[None, None, :, :, None], 0), axis=3)
    begin = jnp.swapaxes(begin, 2, 3)
    nearest = (begin + (q - begin) % NQ) // NQ
    slot = jnp.arange(2, dtype=i32)
    picks = jnp.minimum(nearest[..., None] + slot, local - 1) + local * jnp.arange(NZ, dtype=i32)[:, None]
    packed = pack(shares, picks.reshape(NY * NC * NQ, NZ * 2))
    rows = lax.all_to_all(packed, ("y", "core", "cand"), split_axis=0, concat_axis=0, tiled=True)
    rows = rows.reshape(NY, NC * NQ * NZ * 2, GRAIN, width)
    step = jnp.arange(SPAN, dtype=i32)
    plane = (serve_grain[:, None] + step) % NQ
    from_core, from_z = (dps % NC)[:, None], ((dps // NC) % NZ)[:, None]
    spots = ((from_core * NQ + plane) * NZ + from_z) * 2 + step // NQ

    logits, part = score(rows, spots, serve_block, serve_low, serve_high, centroids)
    norms, own_norms = exchange(own_owner[:, 0], own_owner[:, 1], pick, part, 1)
    updated = update(rows, spots, serve_block, serve_low, serve_high, centroids, logits, norms)

    own = lambda value: lax.dynamic_index_in_dim(value, here, 0, keepdims=False)
    place = jnp.arange(SPAN * GRAIN, dtype=i32)[None, :]
    keep = (place >= own(low)[:, None]) & (place < own(high)[:, None])
    values = jnp.where(keep, own_norms[:, 0, :], 0.0).reshape(listed * SPAN, GRAIN)
    which = (own(grain0)[:, None] + step).reshape(-1)
    spread = (jnp.arange(grains, dtype=i32)[:, None] == which[None, :]).astype(jnp.float32)
    log_partition = jnp.dot(spread, values, precision=lax.Precision.HIGHEST).reshape(row_count)
    return updated, log_partition


def solution(mesh):
    split = Mesh(mesh.devices.reshape(NY, NZ, NC, NQ), ("y", "z", "core", "cand"))
    dp = ("y", "z", "core")
    every = dp + ("cand",)
    return jax.shard_map(
        on_device,
        mesh=split,
        in_specs=(P(dp, None), P(dp), P(), P(), P(every, None, None)),
        out_specs=(P(every, None, None), P(dp)),
        check_vma=False,
    )
```

time: 607 us -> 383 us (0.63)
  other arithmetic: 133 us -> 6.19 us
  Pallas kernels: 0 us -> 74.5 us
  waiting for transfers between devices: 305 us -> 240 us
  matrix products: 48.8 us -> 0.25 us
  starting transfers between devices: 45.8 us -> 7.62 us
  local copies, waits for them, and re-layouts: 53.3 us -> 17.4 us
  between operations: 0.97 us -> 15 us
    all_to_all x5 -> x1, waiting for transfers between devices: 305 us -> 218 us  [on_device(): lax.all_to_all(packed, ('y', 'core', 'cand'), split_axis=0, concat_axis=0...]
    pallas_call x0 -> x4, Pallas kernels: none -> 74.5 us  [the longest x1 26 us: exchange(): pl.pallas_call(exchange_kernel, in_specs=[smem, smem, smem, vmem], out_sp...]
    scatter-add x9 -> x0, other arithmetic: 72.1 us -> none  [the longest x8 71.1 us: accumulate(): return (running.at[block_index].add(partial_value), None)]
    dot_general x9 -> x1, matrix products: 48.8 us -> 0.25 us  [on_device(): jnp.dot(spread, values, precision=lax.Precision.HIGHEST).reshape(row_count)]
    gather x13 -> x3, local copies, waits for them, and re-layouts: 48.4 us -> 6.37 us  [on_device(): slots = jnp.take(block_slots, parent_list, axis=0)]
    all_to_all x5 -> x1, starting transfers between devices: 45.8 us -> 7.58 us  [on_device(): lax.all_to_all(packed, ('y', 'core', 'cand'), split_axis=0, concat_axis=0...]
    all_gather x0 -> x1, waiting for transfers between devices: none -> 21.6 us  [on_device(): shares = lax.all_gather(share, 'z', axis=0, tiled=True)]
    unnamed x0 -> x1, blocking collectives: none -> 21.2 us
  transfers between devices with their start and end apart: 5 -> 2, of which waited for: 3 -> 2; matrix products, arithmetic and copies ran while one was open for 8% -> 5% of each run, Pallas kernels for 0% -> 0%
where the time goes in v1:
time: 383 us; the launch traced here: 382 us
  waiting for transfers between devices  240 us (63%)
  Pallas kernels  74.5 us (19%)
  blocking collectives  21.2 us (6%)
  local copies, waits for them, and re-layouts  17.4 us (5%)
  between operations  15 us (4%)
  starting transfers between devices  7.62 us (2%)
  other arithmetic  6.19 us (2%)
    all_to_all x1, waiting for transfers between devices, on_device(): lax.all_to_all(packed, ('y', 'core', 'cand'), split_axis=0, concat_axis=0...  218 us
    pallas_call x1, Pallas kernels, exchange(): pl.pallas_call(exchange_kernel, in_specs=[smem, smem, smem, vmem], out_sp...  26 us
    all_gather x1, waiting for transfers between devices, on_device(): shares = lax.all_gather(share, 'z', axis=0, tiled=True)  21.6 us
    unnamed x1, blocking collectives  21.2 us
    pallas_call x1, Pallas kernels, pack(): pl.pallas_call(functools.partial(pack_kernel, count), grid_spec=pltpu.Pre...  17.7 us
    pallas_call x1, Pallas kernels, score(): pl.pallas_call(score_kernel, grid_spec=pltpu.PrefetchScalarGridSpec(num_s...  15.6 us
    pallas_call x1, Pallas kernels, update(): pl.pallas_call(update_kernel, grid_spec=pltpu.PrefetchScalarGridSpec(num_...  15.1 us
  transfers between devices with their start and end apart: 2, of which 2 were waited for; matrix products, arithmetic and copies ran while one was open for 5% of the time, Pallas kernels for 0%

profile of v1, /device:TPU:1, one launch (start us, length us, event | category | flops | bytes accessed | tf_op | source)
XLA Modules:
  0.0 382.1 jit_solution(12578464401198617451)
XLA Ops:
  7.2 1.5 copy-done
  8.8 0.8 constant_dynamic-slice_fusion.4
  9.6 0.8 copy.34
  10.4 1.3 dynamic-slice.9
  12.3 0.9 dynamic-slice_reduce_fusion
  13.2 0.9 convert_reduce_fusion
  14.1 0.2 dynamic-update-slice.1
  14.4 21.2 %all-reduce = s32[1024]{0:T(1024)S(1)} all-reduce(s32[1024]{0:T(1024)S(1)} %dynamic-update-slice.1), channel_id=2, replica_groups=mesh['y'=4,'z'=8,'core'=2,'cand'=4] {'y','z','core'}, use_global_device_ids=true, to_apply=%add | all-reduce | flops 1024 | bytes 8192
  35.5 0.1 reshape.231
  35.6 0.1 reshape.225
  35.7 0.2 reduce_window_sum.11
  35.9 0.9 copy.37
  36.8 3.5 gather_fusion
  40.4 1.8 copy.44
  42.1 1.0 copy.40
  43.2 1.0 broadcast_compare_fusion.1
  44.3 0.7 fusion.5
  45.0 0.7 select_reduce_fusion.2
  46.0 0.1 compare_reduce_fusion
  46.1 0.6 select_reduce_fusion
  46.8 0.1 minimum_add_fusion
  46.9 0.7 add.282.pick_ref
  47.6 21.6 %all-gather.4.cloned.1.call-done = bf16[128,1,16,1024]{3,2,1,0:T(8,128)(2,1)} async-done(((bf16[16,1,16,1024]{3,2,1,0:T(8,128)(2,1)}), bf16[128,1,16,1024]{3,2,1,0:T(8,128)(2,1)}) %all-gather.4.cloned.1.call-update) | async-done | bytes 4194320 | tf_op jit(solution)/shard_map/all_gather | solution.py:309
  69.2 17.7 %shard_map.68 = bf16[32,16,16,1024]{3,2,1,0:T(8,128)(2,1)} custom-call(s32[512]{0:T(512)} %add.282.pick_ref, bf16[128,16,1024]{2,1,0:T(8,128)(2,1)} %bitcast.55), custom_call_target="tpu_custom_call" | custom-call | bytes 20971520 | tf_op jit(solution)/shard_map/pallas_call | solution.py:34
  86.9 7.6 %all-to-all-start = ((bf16[32,16,16,1024]{3,2,1,0:T(8,128)(2,1)}), bf16[32,16,16,1024]{3,2,1,0:T(8,128)(2,1)}, u32[]{:S(2)}, u32[]{:S(2)}) async-start(bf16[32,16,16,1024]{3,2,1,0:T(8,128)(2,1)} %shard_map.68), calls=%async_computation | async-start | bytes 33554432 | tf_op jit(solution)/shard_map/all_to_all | solution.py:347
  94.5 0.1 add.259
  94.6 0.1 add.260
  94.7 0.1 add.263
  94.9 0.1 add.246
  95.0 0.1 iota_add_fusion.1
  95.0 0.1 add.288
  95.2 0.1 lt.102
  95.4 0.1 ge.54
  95.5 0.1 iota_add_fusion
  95.6 0.1 add.255
  95.7 0.1 select_reduce_fusion.1.pick_ref
  95.8 0.6 fusion.31.spot_ref
  96.4 218.5 %all-to-all-done = bf16[32,16,16,1024]{3,2,1,0:T(8,128)(2,1)} async-done(((bf16[32,16,16,1024]{3,2,1,0:T(8,128)(2,1)}), bf16[32,16,16,1024]{3,2,1,0:T(8,128)(2,1)}, u32[]{:S(2)}, u32[]{:S(2)}) %all-to-all-start) | async-done | bytes 16777248 | tf_op jit(solution)/shard_map/all_to_all | solution.py:347
  314.9 15.6 %shard_map.69 = (f32[64,128,128]{2,1,0:T(8,128)}, f32[64,2,128]{2,1,0:T(2,128)}) custom-call(s32[512]{0:T(512)} %fusion.31.spot_ref, s32[64]{0:T(128)} %get-tuple-element.27.block_ref, s32[64]{0:T(128)} %get-tuple-element.23.low_ref, s32[64]{0:T(128)} %get-tuple-element.22.high_ref, bf16[4,128,16,1024]{3,2,1,0:T(8,128)(2,1)} %bitcast.11.rows_ref, ...), custom_call_target="tpu_custom_call" | custom-call | flops 1073741824 | bytes 16777216 | tf_op jit(solution)/shard_map/pallas_call | solution.py:123
  330.5 0.8 copy-done.1
  331.4 26.0 %shard_map.70 = (f32[64,1,128]{2,1,0:T(1,128)S(1)}, f32[16,1,128]{2,1,0:T(1,128)S(1)}) custom-call(s32[16]{0:T(128)S(1)} %get-tuple-element.36.first_ref, s32[16]{0:T(128)S(1)} %get-tuple-element.35.second_ref, s32[64]{0:T(128)S(1)} %select_reduce_fusion.1.pick_ref, f32[64,2,128]{2,1,0:T(2,128)S(1)} %copy-done.1), custom_call_target="tpu_custom_call" | custom-call | tf_op jit(solution)/shard_map/pallas_call | solution.py:276
  357.4 0.6 copy-done.2
  357.9 0.5 broadcast.314
  358.5 0.7 reduce.5
  359.1 0.1 squeeze.33
  359.2 0.3 fusion.6
  359.5 0.7 reshape.165
  360.1 15.1 %shard_map.71 = bf16[8,128,1024]{2,1,0:T(8,128)(2,1)} custom-call(s32[512]{0:T(512)} %fusion.31.spot_ref, s32[64]{0:T(128)} %get-tuple-element.27.block_ref, s32[64]{0:T(128)} %get-tuple-element.23.low_ref, s32[64]{0:T(128)} %get-tuple-element.22.high_ref, bf16[4,128,16,1024]{3,2,1,0:T(8,128)(2,1)} %bitcast.11.rows_ref, bf16[8,128,1024]{2,1,0:T(8,128)(2,1)} %cent_ref.3, ...), custom_call_target="tpu_custom_call" | custom-call | flops 1073741824 | bytes 16777216 | tf_op jit(solution)/shard_map/pallas_call | solution.py:152
  (32 shorter events, 0.7 us)
Async XLA Ops:
  7.2 1.6 copy-start
  7.2 62.0 %all-gather.4.cloned.1.call-start = ((), (), s32[]{:S(2)}) async-start(), calls=%async_computation.1 | async-start | bytes 4718592 | tf_op jit(solution)/shard_map/all_gather | solution.py:309
  86.9 228.0 %all-to-all-start = ((bf16[32,16,16,1024]{3,2,1,0:T(8,128)(2,1)}), bf16[32,16,16,1024]{3,2,1,0:T(8,128)(2,1)}, u32[]{:S(2)}, u32[]{:S(2)}) async-start(bf16[32,16,16,1024]{3,2,1,0:T(8,128)(2,1)} %shard_map.68), calls=%async_computation | async-start | bytes 33554432 | tf_op jit(solution)/shard_map/all_to_all | solution.py:347
  330.5 0.8 copy-start.1
  357.3 0.6 copy-start.2
Sparse Core Ops, SparseCore 0:
  10.4 58.7 all-gather.3

commit v2 on v1

v2 whole, which is shorter than its diff:
```python
import functools

import jax
import jax.numpy as jnp
from jax import lax
from jax.experimental import pallas as pl
from jax.experimental.pallas import tpu as pltpu
from jax.sharding import Mesh
from jax.sharding import PartitionSpec as P

sharpness = 3.0
prior_mass = 1.0

GRAIN = 16
SPAN = 8
NY, NZ, NC, NQ = 4, 8, 2, 4
NDP = NY * NZ * NC
PER_Y = NZ * NC
NF = NY * NC
ABREAST = 2
FULL = 2 * PER_Y
ROOMS = (16, 18, 20, 22, FULL)
STEPS = (
    (1, 1), (3, 3), (1, 3), (3, 1), (0, 1), (0, 3), (1, 0), (3, 0),
    (2, 1), (2, 3), (1, 2), (3, 2), (2, 2), (0, 2), (2, 0),
)
MESH = pl.DeviceIdType.MESH
VMEM_LIMIT = 56 * 2**20


def dispatch_kernel(room, pick_ref, grains_ref, rows_ref, send_ref, send_sem, recv_sem, own_sem):
    y, z, c, q = (lax.axis_index(a) for a in ("y", "z", "core", "cand"))
    here = y * NQ + q

    def target(step):
        ty, tq = (y + step[0]) % NY, (q + step[1]) % NQ
        return ty * NQ + tq, (ty, z, c, tq)

    barrier = pltpu.get_barrier_semaphore()
    for step in STEPS:
        pl.semaphore_signal(barrier, 1, device_id=target(step)[1], device_id_type=MESH)
    pl.semaphore_wait(barrier, len(STEPS))

    def copy(n, places):
        index, device = target(STEPS[n])
        return pltpu.make_async_remote_copy(
            send_ref.at[index, places], rows_ref.at[here, places], send_sem.at[n], recv_sem.at[n],
            device_id=device, device_id_type=MESH,
        )

    @pl.loop(0, room)
    def _(place):
        for n, step in enumerate(STEPS):
            index, _ = target(step)
            send_ref[index, place] = grains_ref[pick_ref[index * FULL + place]]
            copy(n, pl.ds(place, 1)).start()
        send_ref[here, place] = grains_ref[pick_ref[here * FULL + place]]

    every = pl.ds(0, room)
    kept = pltpu.make_async_copy(send_ref.at[here, every], rows_ref.at[here, every], own_sem)
    kept.start()
    kept.wait()
    for n in range(len(STEPS)):
        copy(n, every).wait()


def dispatch(room, collective_id, grains, picks):
    targets = picks.shape[0]
    shape = grains.shape[1:]
    return pl.pallas_call(
        functools.partial(dispatch_kernel, room),
        in_specs=[pl.BlockSpec(memory_space=pltpu.SMEM), pl.BlockSpec(memory_space=pltpu.VMEM)],
        out_specs=pl.BlockSpec(memory_space=pl.ANY),
        out_shape=jax.ShapeDtypeStruct((targets, FULL) + shape, grains.dtype),
        scratch_shapes=[
            pltpu.VMEM((targets, room) + shape, grains.dtype),
            pltpu.SemaphoreType.DMA((len(STEPS),)),
            pltpu.SemaphoreType.DMA((len(STEPS),)),
            pltpu.SemaphoreType.DMA,
        ],
        compiler_params=pltpu.CompilerParams(
            collective_id=collective_id, has_side_effects=True, vmem_limit_bytes=VMEM_LIMIT
        ),
        cost_estimate=pl.CostEstimate(
            flops=0, bytes_accessed=2 * (grains.size + targets * room * shape[0] * shape[1]), transcendentals=0
        ),
    )(picks.reshape(-1), grains)


def window_rows(rows_ref, spot_ref, window):
    parts = [rows_ref[0, spot_ref[window * SPAN + k]] for k in range(SPAN)]
    return jnp.concatenate(parts, axis=0)


def by_core(i):
    return (i % NC) * NZ + i // NC


def score_kernel(spot_ref, block_ref, order_ref, many_ref, rows_ref, cent_ref, logit_ref, part_ref, square_ref):
    group = pl.program_id(0)

    @pl.when(group == 0)
    def _():
        @pl.loop(0, cent_ref.shape[0])
        def _(b):
            wide = cent_ref[b].astype(jnp.float32)
            square_ref[b] = jnp.sum(wide * wide, axis=1, keepdims=True)

    @pl.loop(0, (many_ref[group] + ABREAST - 1) // ABREAST)
    def _(step):
        places = [order_ref[group * PER_Y + step * ABREAST + n] for n in range(ABREAST)]
        results = []
        for i in places:
            window = group * PER_Y + i
            rows = window_rows(rows_ref, spot_ref, window)
            b = block_ref[window]
            scores = lax.dot_general(
                cent_ref[b], rows, (((1,), (1,)), ((), ())), preferred_element_type=jnp.float32
            )
            logits = sharpness * (scores - 0.5 * square_ref[b])
            highest = jnp.max(logits, axis=0, keepdims=True)
            total = jnp.sum(jnp.exp(logits - highest), axis=0, keepdims=True)
            results.append((logits, jnp.concatenate([highest, total], axis=0)))
        for i, (logits, part) in zip(places, results):
            logit_ref[i] = logits
            part_ref[by_core(i)] = part


def update_kernel(
    spot_ref, block_ref, low_ref, high_ref, order_ref, many_ref,
    rows_ref, cent_ref, logit_ref, norm_ref, out_ref, sum_ref, mass_ref,
):
    group = pl.program_id(0)

    @pl.when(group == 0)
    def _():
        sum_ref[...] = jnp.zeros_like(sum_ref)
        mass_ref[...] = jnp.zeros_like(mass_ref)

    @pl.loop(0, (many_ref[group] + ABREAST - 1) // ABREAST)
    def _(step):
        results = []
        for n in range(ABREAST):
            i = order_ref[group * PER_Y + step * ABREAST + n]
            window = group * PER_Y + i
            rows = window_rows(rows_ref, spot_ref, window)
            place = lax.broadcasted_iota(jnp.int32, logit_ref.shape[1:], 1)
            keep = (place >= low_ref[window]) & (place < high_ref[window])
            weights = jnp.where(keep, jnp.exp(logit_ref[i] - norm_ref[by_core(i)]), 0.0).astype(jnp.bfloat16)
            sums = lax.dot_general(weights, rows, (((1,), (0,)), ((), ())), preferred_element_type=jnp.float32)
            mass = jnp.sum(weights.astype(jnp.float32), axis=1, keepdims=True)
            results.append((block_ref[window], sums, mass))
        for b, sums, mass in results:
            sum_ref[b] += sums
            mass_ref[b] += mass

    @pl.when(group == NY - 1)
    def _():
        @pl.loop(0, cent_ref.shape[0])
        def _(b):
            new = (sum_ref[b] + prior_mass * cent_ref[b].astype(jnp.float32)) / (mass_ref[b] + prior_mass)
            out_ref[b] = new.astype(out_ref.dtype)


def score(rows, spots, serving, centroids):
    stored, lanes, width = centroids.shape
    span = SPAN * GRAIN
    block, _, _, order, many = serving
    return pl.pallas_call(
        score_kernel,
        grid_spec=pltpu.PrefetchScalarGridSpec(
            num_scalar_prefetch=4,
            grid=(NY,),
            in_specs=[
                pl.BlockSpec((1,) + rows.shape[1:], lambda g, *_: (g, 0, 0, 0)),
                pl.BlockSpec(centroids.shape, lambda g, *_: (0, 0, 0)),
            ],
            out_specs=[
                pl.BlockSpec((PER_Y, lanes, span), lambda g, *_: (g, 0, 0)),
                pl.BlockSpec((PER_Y, 2, span), lambda g, *_: (g, 0, 0)),
            ],
            scratch_shapes=[pltpu.VMEM((stored, lanes, 1), jnp.float32)],
        ),
        out_shape=[
            jax.ShapeDtypeStruct((NDP, lanes, span), jnp.float32),
            jax.ShapeDtypeStruct((NDP, 2, span), jnp.float32),
        ],
        compiler_params=pltpu.CompilerParams(vmem_limit_bytes=VMEM_LIMIT),
        cost_estimate=pl.CostEstimate(
            flops=NDP * lanes * span * width, bytes_accessed=2 * rows.size, transcendentals=NDP * lanes * span
        ),
    )(spots.reshape(-1), block, order, many, rows, centroids)


def update(rows, spots, serving, centroids, logits, norms):
    stored, lanes, width = centroids.shape
    span = SPAN * GRAIN
    return pl.pallas_call(
        update_kernel,
        grid_spec=pltpu.PrefetchScalarGridSpec(
            num_scalar_prefetch=6,
            grid=(NY,),
            in_specs=[
                pl.BlockSpec((1,) + rows.shape[1:], lambda g, *_: (g, 0, 0, 0)),
                pl.BlockSpec(centroids.shape, lambda g, *_: (0, 0, 0)),
                pl.BlockSpec((PER_Y, lanes, span), lambda g, *_: (g, 0, 0)),
                pl.BlockSpec((PER_Y, 1, span), lambda g, *_: (g, 0, 0)),
            ],
            out_specs=pl.BlockSpec(centroids.shape, lambda g, *_: (0, 0, 0)),
            scratch_shapes=[
                pltpu.VMEM((stored, lanes, width), jnp.float32),
                pltpu.VMEM((stored, lanes, 1), jnp.float32),
            ],
        ),
        out_shape=jax.ShapeDtypeStruct(centroids.shape, centroids.dtype),
        compiler_params=pltpu.CompilerParams(vmem_limit_bytes=VMEM_LIMIT),
        cost_estimate=pl.CostEstimate(
            flops=NDP * lanes * span * width, bytes_accessed=2 * rows.size, transcendentals=NDP * lanes * span
        ),
    )(spots.reshape(-1), *serving, rows, centroids, logits, norms)


def joint(former, latter):
    highest = jnp.maximum(former[0:1], latter[0:1])
    total = former[1:2] * jnp.exp(former[0:1] - highest) + latter[1:2] * jnp.exp(latter[0:1] - highest)
    return jnp.concatenate([highest, total], axis=0)


def exchange_kernel(
    first_ref, second_ref, pick_ref, part_ref, got_ref, own_ref,
    flat_ref, deep_ref, half_ref, quarters_ref, send_ref, fore_ref, land_ref,
    send_sem, recv_sem,
):
    y, z, c, q = (lax.axis_index(a) for a in ("y", "z", "core", "cand"))
    flat = y * NC + c
    listed = own_ref.shape[0]

    def across(step):
        peer = (flat + step) % NF
        return peer, (peer // NC, z, peer % NC, q)

    def along(step):
        peer = (z + step) % NZ
        return peer, (y, peer, c, q)

    def crossing(step):
        return (y, z, c, (q + step) % NQ)

    def start(kind, step, source, target, device):
        copy = pltpu.make_async_remote_copy(
            source, target, send_sem.at[kind, step], recv_sem.at[kind, step], device_id=device, device_id_type=MESH
        )
        copy.start()
        return copy

    barrier = pltpu.get_barrier_semaphore()
    for step in range(1, NF):
        pl.semaphore_signal(barrier, 1, device_id=across(step)[1], device_id_type=MESH)
    for step in range(1, NZ):
        pl.semaphore_signal(barrier, 1, device_id=along(step)[1], device_id_type=MESH)
    for step in range(1, NQ):
        pl.semaphore_signal(barrier, 1, device_id=crossing(step), device_id_type=MESH)
    pl.semaphore_wait(barrier, NF - 1 + NZ - 1 + NQ - 1)

    copies = []
    for step in range(1, NF):
        peer, device = across(step)
        copies.append(start(0, step, part_ref.at[peer], flat_ref.at[:, flat], device))
    flat_ref[:, flat] = part_ref[flat]
    for copy in copies:
        copy.wait()
    copies = []
    for step in range(1, NZ):
        peer, device = along(step)
        copies.append(start(1, step, flat_ref.at[peer], deep_ref.at[z], device))
    deep_ref[z] = flat_ref[z]
    for copy in copies:
        copy.wait()

    for e in range(listed):
        one, two = first_ref[e], second_ref[e]
        half_ref[e] = joint(deep_ref[one // NF, one % NF], deep_ref[two // NF, two % NF])
    copies = [start(2, step, half_ref, quarters_ref.at[step], crossing(step)) for step in range(1, NQ)]
    for copy in copies:
        copy.wait()
    for e in range(listed):
        both = joint(half_ref[e], quarters_ref[1, e])
        rest = joint(quarters_ref[2, e], quarters_ref[3, e])
        pair = joint(both, rest)
        own_ref[e] = pair[0:1] + jnp.log(pair[1:2])

    for zj in range(NZ):
        for fj in range(NF):
            send_ref[zj, fj] = own_ref[pick_ref[zj * NF + fj]]
    copies = []
    for step in range(1, NZ):
        peer, device = along(step)
        copies.append(start(3, step, send_ref.at[peer], fore_ref.at[:, z], device))
    fore_ref[:, z] = send_ref[z]
    for copy in copies:
        copy.wait()
    copies = []
    for step in range(1, NF):
        peer, device = across(step)
        copies.append(start(4, step, fore_ref.at[peer], land_ref.at[flat], device))
    land_ref[flat] = fore_ref[flat]
    for copy in copies:
        copy.wait()
    got_ref[...] = land_ref[...]


def exchange(first, second, pick, part, collective_id):
    listed = first.shape[0]
    span = SPAN * GRAIN
    smem, vmem = pl.BlockSpec(memory_space=pltpu.SMEM), pl.BlockSpec(memory_space=pltpu.VMEM)
    buffer = lambda *shape: pltpu.VMEM(shape + (span,), jnp.float32)
    got, own = pl.pallas_call(
        exchange_kernel,
        in_specs=[smem, smem, smem, vmem],
        out_specs=[vmem, vmem],
        out_shape=[
            jax.ShapeDtypeStruct((NF, NZ, 1, span), jnp.float32),
            jax.ShapeDtypeStruct((listed, 1, span), jnp.float32),
        ],
        scratch_shapes=[
            buffer(NZ, NF, 2), buffer(NZ, NF, 2), buffer(listed, 2), buffer(NQ, listed, 2),
            buffer(NZ, NF, 1), buffer(NF, NZ, 1), buffer(NF, NZ, 1),
            pltpu.SemaphoreType.DMA((5, NZ)), pltpu.SemaphoreType.DMA((5, NZ)),
        ],
        compiler_params=pltpu.CompilerParams(
            collective_id=collective_id, has_side_effects=True, vmem_limit_bytes=16 * 2**20
        ),
    )(first, second, pick, part.reshape(NF, NZ, 2, span))
    return got.reshape(NDP, 1, span), own


def on_device(embeddings, point_parent, parent_list, block_slots, centroids):
    y, z, c, q = (lax.axis_index(a) for a in ("y", "z", "core", "cand"))
    here = (y * NZ + z) * NC + c
    row_count, width = embeddings.shape
    stored = centroids.shape[0]
    listed = parent_list.shape[1]
    grains = row_count // GRAIN
    local = grains // NQ
    i32 = jnp.int32

    share = lax.dynamic_index_in_dim(embeddings.reshape(local, NQ, GRAIN, width), q, 1, keepdims=False)
    shares = lax.all_gather(share, ("z", "core"), axis=0, tiled=True)

    counts = jnp.sum((point_parent[:, None] == parent_list[here][None, :]).astype(i32), axis=0)
    counts = lax.all_gather(counts, ("y", "z", "core"), axis=0)
    starts = jnp.cumsum(counts, axis=1) - counts
    begin = starts // GRAIN
    last = (starts + counts - 1) // GRAIN
    low = starts % GRAIN
    high = low + counts
    slots = jnp.take(block_slots, parent_list, axis=0)
    owner = slots // (stored * NQ)
    planes = jnp.arange(NQ, dtype=i32)

    def share_of(begin, last, plane):
        nearest = begin + (plane - begin) % NQ
        return nearest, (nearest <= last).astype(i32) + (nearest + NQ <= last).astype(i32)

    loads = share_of(begin[..., None], last[..., None], planes)[1]
    loads = jnp.broadcast_to(loads[:, :, None, :], (NDP, listed, 2, NQ)).reshape(NY, PER_Y * listed * 2, NQ)
    takers = jnp.swapaxes(owner, 2, 3).reshape(NY, PER_Y * listed * 2, NQ)
    takes = takers[..., None] == jnp.arange(NDP, dtype=i32)
    totals = jnp.einsum(
        "ymqj,ymp->yqjp", takes.astype(jnp.bfloat16), loads.astype(jnp.bfloat16), preferred_element_type=jnp.float32
    )
    size = jnp.sum((jnp.max(totals) > jnp.asarray(ROOMS[:-1], jnp.float32)).astype(i32))

    mine = jnp.take(owner, q, axis=2) == here
    entry = jnp.any(mine, axis=2)
    chosen = lambda value: jnp.sum(jnp.where(entry, value, 0), axis=1)
    served = jnp.any(entry, axis=1)
    serve_low, serve_high, serve_begin = chosen(low), chosen(high), chosen(begin)
    serve_last = jnp.where(served, chosen(last), -1)
    serve_block = jnp.sum(jnp.where(mine, jnp.take(slots, q, axis=2) % stored, 0), axis=(1, 2))
    grouped = served.reshape(NY, PER_Y).astype(i32)
    many = jnp.sum(grouped, axis=1)
    rank = jnp.where(
        grouped > 0, jnp.cumsum(grouped, axis=1) - 1, many[:, None] + jnp.cumsum(1 - grouped, axis=1) - 1
    )
    around = jnp.arange(PER_Y, dtype=i32)
    order = jnp.sum(jnp.where(rank[:, :, None] == around, around[None, :, None], 0), axis=1).reshape(-1)
    serving = (serve_block, serve_low, serve_high, order, many)

    _, landing = share_of(serve_begin[:, None], serve_last[:, None], planes)
    landing = landing.reshape(NY, PER_Y, NQ)
    base = (jnp.cumsum(landing, axis=1) - landing).reshape(NDP, NQ)
    step = jnp.arange(SPAN, dtype=i32)
    grain = serve_begin[:, None] + step
    plane = grain % NQ
    within = jnp.sum(jnp.where(plane[..., None] == planes, base[:, None, :], 0), axis=2) + step // NQ
    real = grain <= serve_last[:, None]
    within = jnp.where(real, within, within[:, :1])
    plane = jnp.where(real, plane, plane[:, :1])
    within = jnp.where(served[:, None], within, 0)

    own = lambda value: lax.dynamic_index_in_dim(value, here, 0, keepdims=False)
    dps = jnp.arange(NDP, dtype=i32)
    by_layer = dps.reshape(NY, NZ, NC).transpose(1, 0, 2).reshape(-1)
    own_owner = own(jnp.take(owner, q, axis=2))
    pick = jnp.sum(
        jnp.where(own_owner[None] == by_layer[:, None, None], jnp.arange(listed, dtype=i32)[None, :, None], 0),
        axis=(1, 2),
    )
    deep = lambda index: (index // NC % NZ) * NF + (index // PER_Y) * NC + index % NC

    of_y = lambda value: lax.dynamic_index_in_dim(value.reshape((NY, PER_Y) + value.shape[1:]), y, 0, keepdims=False)
    target = (jnp.arange(NY, dtype=i32) * NZ + z) * NC + c
    hit = jnp.any(of_y(owner)[None] == target[:, None, None, None, None], axis=-1)
    sent = lambda value: jnp.sum(jnp.where(hit, of_y(value)[None, :, :, None], 0), axis=2)
    nearest, sending = share_of(sent(begin), jnp.where(jnp.any(hit, axis=2), sent(last), -1), q)
    place = jnp.cumsum(sending, axis=1) - sending
    room = jnp.arange(FULL, dtype=i32)
    picks = 0
    for slot in range(2):
        here_now = (place[..., None] + slot == room) & (sending[..., None] > slot)
        which = around[:, None] * local + nearest // NQ + slot
        picks = picks + jnp.sum(jnp.where(here_now, which[..., None], 0), axis=1)
    picks = picks.reshape(NY * NQ, FULL)

    branches = [functools.partial(dispatch, room, 2 + n) for n, room in enumerate(ROOMS)]
    rows = lax.switch(size, branches, shares, picks)
    rows = rows.reshape(NY, NQ * FULL, GRAIN, width)
    spots = plane * FULL + within
    logits, part = score(rows, spots, serving, centroids)
    norms, own_norms = exchange(deep(own_owner[:, 0]), deep(own_owner[:, 1]), pick, part, 1)
    updated = update(rows, spots, serving, centroids, logits, norms)

    place = jnp.arange(SPAN * GRAIN, dtype=i32)[None, :]
    keep = (place >= own(low)[:, None]) & (place < own(high)[:, None])
    values = jnp.where(keep, own_norms[:, 0, :], 0.0).reshape(listed * SPAN, GRAIN)
    which = (own(begin)[:, None] + step).reshape(-1)
    spread = (jnp.arange(grains, dtype=i32)[:, None] == which[None, :]).astype(jnp.float32)
    log_partition = jnp.dot(spread, values, precision=lax.Precision.HIGHEST).reshape(row_count)
    return updated, log_partition


def solution(mesh):
    split = Mesh(mesh.devices.reshape(NY, NZ, NC, NQ), ("y", "z", "core", "cand"))
    dp = ("y", "z", "core")
    every = dp + ("cand",)
    return jax.shard_map(
        on_device,
        mesh=split,
        in_specs=(P(dp, None), P(dp), P(), P(), P(every, None, None)),
        out_specs=(P(every, None, None), P(dp)),
        check_vma=False,
    )
```

time: 383 us -> 253 us (0.66)
  waiting for transfers between devices: 240 us -> 2.63 us
  Pallas kernels: 74.5 us -> 167 us
  local copies, waits for them, and re-layouts: 17.4 us -> 28.2 us
  other arithmetic: 6.19 us -> 15.3 us
  starting transfers between devices: 7.62 us -> 0.04 us
    all_to_all x1 -> x0, waiting for transfers between devices: 218 us -> none  [on_device(): lax.all_to_all(packed, ('y', 'core', 'cand'), split_axis=0, concat_axis=0...]
    pallas_call x1, Pallas kernels: 17.7 us -> 112 us  [dispatch(): pl.pallas_call(functools.partial(dispatch_kernel, room), in_specs=[pl.Blo...]
    all_gather x1, waiting for transfers between devices: 21.6 us -> 2.62 us  [on_device(): shares = lax.all_gather(share, ('z', 'core'), axis=0, tiled=True)]
    all_to_all x1 -> x0, starting transfers between devices: 7.58 us -> none  [on_device(): lax.all_to_all(packed, ('y', 'core', 'cand'), split_axis=0, concat_axis=0...]
  transfers between devices with their start and end apart: 2 -> 1, of which waited for: 2 -> 1; matrix products, arithmetic and copies ran while one was open for 5% -> 14% of each run, Pallas kernels for 0% -> 0%
where the time goes in v2:
time: 253 us; the launch traced here: 252 us
  Pallas kernels  167 us (66%)
  local copies, waits for them, and re-layouts  28.2 us (11%)
  blocking collectives  21.2 us (8%)
  between operations  15.8 us (6%)
  other arithmetic  15.3 us (6%)
  waiting for transfers between devices  2.63 us (1%)
    pallas_call x1, Pallas kernels, dispatch(): pl.pallas_call(functools.partial(dispatch_kernel, room), in_specs=[pl.Blo...  112 us
    pallas_call x1, Pallas kernels, exchange(): pl.pallas_call(exchange_kernel, in_specs=[smem, smem, smem, vmem], out_sp...  27.9 us
    unnamed x1, blocking collectives  21.2 us
    pallas_call x1, Pallas kernels, update(): pl.pallas_call(update_kernel, grid_spec=pltpu.PrefetchScalarGridSpec(num_...  13.4 us
    pallas_call x1, Pallas kernels, score(): pl.pallas_call(score_kernel, grid_spec=pltpu.PrefetchScalarGridSpec(num_s...  13.2 us
    gather x3, local copies, waits for them, and re-layouts, on_device(): slots = jnp.take(block_slots, parent_list, axis=0)  6.46 us
    unnamed x21, local copies, waits for them, and re-layouts  6.16 us
  transfers between devices with their start and end apart: 1, of which 1 were waited for; matrix products, arithmetic and copies ran while one was open for 14% of the time, Pallas kernels for 0%

profile of v2, /device:TPU:1, one launch (start us, length us, event | category | flops | bytes accessed | tf_op | source)
XLA Modules:
  0.0 251.8 jit_solution(15274123447836938986)
XLA Ops:
  7.2 1.5 copy-done
  8.8 0.8 constant_dynamic-slice_fusion.4
  9.7 0.7 reshape.559
  10.3 0.8 copy.164
  11.1 1.3 dynamic-slice.5
  13.0 0.9 dynamic-slice_reduce_fusion
  13.9 0.9 convert_reduce_fusion
  15.1 21.2 %all-reduce = s32[1024]{0:T(1024)S(1)} all-reduce(s32[1024]{0:T(1024)S(1)} %dynamic-update-slice.1), channel_id=2, replica_groups=mesh['y'=4,'z'=8,'core'=2,'cand'=4] {'y','z','core'}, use_global_device_ids=true, to_apply=%add | all-reduce | flops 1024 | bytes 8192
  36.6 0.9 copy.167
  37.5 3.5 %gather_fusion = s32[1024,4,2]{1,2,0:T(2,128)S(1)} fusion(s32[256,4,2]{1,2,0:T(2,128)S(1)} %copy.167, s32[1024]{0:T(1024)S(1)} %broadcast_clamp_fusion), kind=kCustom, calls=%fused_computation | custom fusion | bytes 69632 | tf_op jit(solution)/shard_map/jit(_take)/gather | solution.py:357
  41.0 1.8 copy.208
  42.8 1.1 copy.175
  44.0 1.1 add_select_fusion.1
  45.2 1.3 fusion.21
  47.4 0.6 reshape.550.order_ref
  48.1 0.6 broadcast_in_dim.290
  48.7 1.3 select_reduce_fusion.14
  50.3 0.7 add.587
  51.0 0.6 lt.126
  51.7 0.7 ge.54
  53.4 0.7 le.112
  54.2 0.7 broadcast_in_dim.288
  55.5 0.6 select_reduce_fusion.11
  56.3 0.8 copy.177
  57.1 1.0 copy.172
  58.4 1.3 add_convert_fusion
  60.1 1.2 fusion.2
  61.3 2.0 fusion.61
  63.9 0.7 constant_dynamic-slice_fusion.3
  64.7 0.8 select_reduce_fusion.12.pick_ref
  65.5 1.3 fusion.58.spot_ref
  66.8 1.2 fusion.14
  68.1 2.6 %all-gather.4.cloned.1.call-done = bf16[256,1,16,1024]{3,2,1,0:T(8,128)(2,1)} async-done(((bf16[16,1,16,1024]{3,2,1,0:T(8,128)(2,1)}), bf16[256,1,16,1024]{3,2,1,0:T(8,128)(2,1)}) %all-gather.4.cloned.1.call-update) | async-done | bytes 8388624 | tf_op jit(solution)/shard_map/all_gather | solution.py:348
  70.8 116.0 %conditional.1 = (bf16[4,128,16,1024]{3,2,1,0:T(8,128)(2,1)}) conditional(s32[]{:T(128)} %clamp.3, (s32[4,16,4,1]{3,2,1,0:T(4,128)S(1)}, s32[4,16,4,32]{3,2,1,0:T(4,128)S(1)}, s32[4,16,4,1]{3,2,1,0:T(4,128)S(1)}, s32[4,16,4,1]{3,2,1,0:T(4,128)S(1)}, s32[4,16,4,1]{3,2,1,0:T(4,128)S(1)}, ...), branch_computations={%region_22.26_spmd, %region_25.29_spmd, %region_28.32_spmd, %regio... | conditional | flops 66048 | bytes 25305096 | solution.py:427
  71.3 0.5 copy.188
  71.9 0.5 copy.187
  72.4 0.5 copy.186
  72.9 0.6 select_reduce_fusion.2
  73.5 0.7 add.453.pick_ref
  74.1 112.4 %branch_1_fun.2 = bf16[16,32,16,1024]{3,2,1,0:T(8,128)(2,1)} custom-call(s32[512]{0:T(512)} %add.453.pick_ref, bf16[256,16,1024]{2,1,0:T(8,128)(2,1)} %get-tuple-element.425.grains_ref), custom_call_target="tpu_custom_call" | custom-call | bytes 17825792 | tf_op jit(solution)/shard_map/cond/branch_1_fun/pallas_call | solution.py:70
  186.8 13.2 %shard_map.77 = (f32[64,128,128]{2,1,0:T(8,128)}, f32[64,2,128]{2,1,0:T(2,128)}) custom-call(s32[512]{0:T(512)} %fusion.58.spot_ref, s32[64]{0:T(128)} %get-tuple-element.678.block_ref, s32[64]{0:T(128)} %reshape.550.order_ref, s32[4]{0:T(128)} %copy-done.4, bf16[4,128,16,1024]{3,2,1,0:T(8,128)(2,1)} %get-tuple-element.708.rows_ref, ...), custom_call_target="tpu_custom_call" | custom-call | flops 1073741824 | bytes 16777216 | tf_op jit(solution)/shard_map/pallas_call | solution.py:169
  200.0 0.8 copy-done.1
  200.8 27.9 %shard_map.78 = (f32[8,8,1,128]{3,2,1,0:T(1,128)S(1)}, f32[16,1,128]{2,1,0:T(1,128)S(1)}) custom-call(s32[16]{0:T(128)S(1)} %get-tuple-element.701.first_ref, s32[16]{0:T(128)S(1)} %get-tuple-element.700.second_ref, s32[64]{0:T(128)S(1)} %select_reduce_fusion.12.pick_ref, f32[8,8,2,128]{3,2,1,0:T(2,128)S(1)} %bitcast.157), custom_call_target="tpu_custom_call" | custom-call | tf_op jit(solution)/shard_map/pallas_call | solution.py:317
  228.7 0.6 copy-done.2
  229.3 0.5 broadcast.828
  229.8 0.7 reduce.7
  230.8 0.7 reshape.562
  231.5 13.4 %shard_map.79 = bf16[8,128,1024]{2,1,0:T(8,128)(2,1)} custom-call(s32[512]{0:T(512)} %fusion.58.spot_ref, s32[64]{0:T(128)} %get-tuple-element.678.block_ref, s32[64]{0:T(128)} %get-tuple-element.671.low_ref, s32[64]{0:T(128)} %get-tuple-element.670.high_ref, s32[64]{0:T(128)} %reshape.550.order_ref, s32[4]{0:T(128)} %copy-done.4, ...), custom_call_target="tpu_custom_call" | custom-call | flops 1073741824 | bytes 16777216 | tf_op jit(solution)/shard_map/pallas_call | solution.py:198
  (91 shorter events, 5.6 us)
Async XLA Ops:
  7.2 1.6 copy-start
  7.2 63.5 %all-gather.4.cloned.1.call-start = ((), (), s32[]{:S(2)}) async-start(), calls=%async_computation | async-start | bytes 8912896 | tf_op jit(solution)/shard_map/all_gather | solution.py:348
  47.0 21.1 %copy-start.4 = (s32[4]{0:T(128)}, s32[4]{0:T(128)S(1)}, u32[]{:S(2)}) copy-start(s32[4]{0:T(128)S(1)} %get-tuple-element.698.many_ref) | copy-start | bytes 52
  50.0 6.1 %copy-start.3 = (s32[64,16]{1,0:T(8,128)}, s32[64,16]{1,0:T(8,128)S(1)}, u32[]{:S(2)}) copy-start(s32[64,16]{1,0:T(8,128)S(1)} %get-tuple-element.681) | copy-start | bytes 12292
  186.8 43.8 %copy-start.5 = (s32[128]{0:T(128)S(1)}, s32[128]{0:T(128)}, u32[]{:S(2)}) copy-start(s32[128]{0:T(128)} %add.587) | copy-start | bytes 1540
  186.8 43.8 %copy-start.6 = (s32[128]{0:T(128)S(1)}, s32[128]{0:T(128)}, u32[]{:S(2)}) copy-start(s32[128]{0:T(128)} %lt.126) | copy-start | bytes 1540
  186.8 43.8 %copy-start.7 = (s32[128]{0:T(128)S(1)}, s32[128]{0:T(128)}, u32[]{:S(2)}) copy-start(s32[128]{0:T(128)} %ge.54) | copy-start | bytes 1540
  200.0 0.8 copy-start.1
  228.7 0.6 copy-start.2
Sparse Core Ops, SparseCore 0:
  10.4 60.2 all-gather.3

commit v3 on v2

v3 whole, which is shorter than its diff:
```python
import functools

import jax
import jax.numpy as jnp
from jax import lax
from jax.experimental import pallas as pl
from jax.experimental.pallas import tpu as pltpu
from jax.sharding import Mesh
from jax.sharding import PartitionSpec as P

sharpness = 3.0
prior_mass = 1.0

GRAIN = 16
SPAN = 8
NY, NZ, NC, NQ = 4, 8, 2, 4
NDP = NY * NZ * NC
PER_Y = NZ * NC
ABREAST = 4
FULL = 2 * PER_Y
ROOMS = (16, 17, 18, 19, 20, 21, 23, FULL)
STEPS = (
    (1, 1), (3, 3), (1, 3), (3, 1), (0, 1), (0, 3), (1, 0), (3, 0),
    (2, 1), (2, 3), (1, 2), (3, 2), (2, 2), (0, 2), (2, 0),
)
PIECES = (0, 16, 18, 20, 23, FULL)
MESH = pl.DeviceIdType.MESH
VMEM_LIMIT = 56 * 2**20


def dispatch_kernel(room, pick_ref, share_ref, rows_ref, grains_ref, send_ref, send_sem, recv_sem, own_sem):
    y, z, c, q = (lax.axis_index(a) for a in ("y", "z", "core", "cand"))
    here = y * NQ + q

    def target(step):
        ty, tq = (y + step[0]) % NY, (q + step[1]) % NQ
        return ty * NQ + tq, (ty, z, c, tq)

    load = pltpu.make_async_copy(share_ref, grains_ref, own_sem.at[0])
    load.start()
    barrier = pltpu.get_barrier_semaphore()
    for step in STEPS:
        pl.semaphore_signal(barrier, 1, device_id=target(step)[1], device_id_type=MESH)
    pl.semaphore_wait(barrier, len(STEPS))
    load.wait()

    def copy(n, places):
        index, device = target(STEPS[n])
        return pltpu.make_async_remote_copy(
            send_ref.at[index, places], rows_ref.at[here, places], send_sem.at[n], recv_sem.at[n],
            device_id=device, device_id_type=MESH,
        )

    @pl.loop(0, room)
    def _(place):
        for n, step in enumerate(STEPS):
            index, _ = target(step)
            send_ref[index, place] = grains_ref[pick_ref[index * FULL + place]]
            copy(n, pl.ds(place, 1)).start()
        send_ref[here, place] = grains_ref[pick_ref[here * FULL + place]]

    every = pl.ds(0, room)
    kept = pltpu.make_async_copy(send_ref.at[here, every], rows_ref.at[here, every], own_sem.at[1])
    kept.start()
    for n in range(len(STEPS)):
        copy(n, every).wait()
    kept.wait()


def dispatch(room, collective_id, grains, picks):
    targets = picks.shape[0]
    shape = grains.shape[1:]
    return pl.pallas_call(
        functools.partial(dispatch_kernel, room),
        in_specs=[pl.BlockSpec(memory_space=pltpu.SMEM), pl.BlockSpec(memory_space=pl.ANY)],
        out_specs=pl.BlockSpec(memory_space=pl.ANY),
        out_shape=jax.ShapeDtypeStruct((targets, FULL) + shape, grains.dtype),
        scratch_shapes=[
            pltpu.VMEM(grains.shape, grains.dtype),
            pltpu.VMEM((targets, room) + shape, grains.dtype),
            pltpu.SemaphoreType.DMA((len(STEPS),)),
            pltpu.SemaphoreType.DMA((len(STEPS),)),
            pltpu.SemaphoreType.DMA((2,)),
        ],
        compiler_params=pltpu.CompilerParams(
            collective_id=collective_id, has_side_effects=True, vmem_limit_bytes=VMEM_LIMIT
        ),
        cost_estimate=pl.CostEstimate(
            flops=0, bytes_accessed=2 * (grains.size + targets * room * shape[0] * shape[1]), transcendentals=0
        ),
    )(picks.reshape(-1), grains)


def by_core(i):
    return (i % NC) * NZ + i // NC


def fetch(room_ref, rows_ref, held_ref, sems, group, act):
    for n, (begin, end) in enumerate(zip(PIECES, PIECES[1:])):
        places = pl.ds(begin, end - begin)

        @pl.when(room_ref[0] > begin)
        def _():
            act(
                pltpu.make_async_copy(
                    rows_ref.at[group, :, places], held_ref.at[group, :, places], sems.at[group, n]
                )
            )


def window_rows(held_ref, spot_ref, group, window):
    spots = [spot_ref[window * SPAN + k] for k in range(SPAN)]
    return jnp.concatenate([held_ref[group, spot // FULL, spot % FULL] for spot in spots], axis=0)


def score_kernel(
    spot_ref, block_ref, order_ref, many_ref, room_ref, rows_ref, cent_ref, logit_ref, part_ref,
    held_ref, kept_ref, square_ref, in_sem, out_sem,
):
    for group in range(NY):
        fetch(room_ref, rows_ref, held_ref, in_sem, group, lambda copy: copy.start())

    @pl.loop(0, cent_ref.shape[0])
    def _(b):
        wide = cent_ref[b].astype(jnp.float32)
        square_ref[b] = jnp.sum(wide * wide, axis=1, keepdims=True)

    def out(group):
        windows = pl.ds(group * PER_Y, PER_Y)
        return pltpu.make_async_copy(kept_ref.at[windows], logit_ref.at[windows], out_sem.at[group])

    for group in range(NY):
        fetch(room_ref, rows_ref, held_ref, in_sem, group, lambda copy: copy.wait())

        @pl.loop(0, (many_ref[group] + ABREAST - 1) // ABREAST)
        def _(step):
            places = [order_ref[group * PER_Y + step * ABREAST + n] for n in range(ABREAST)]
            results = []
            for i in places:
                window = group * PER_Y + i
                rows = window_rows(held_ref, spot_ref, group, window)
                b = block_ref[window]
                scores = lax.dot_general(
                    cent_ref[b], rows, (((1,), (1,)), ((), ())), preferred_element_type=jnp.float32
                )
                logits = sharpness * (scores - 0.5 * square_ref[b])
                highest = jnp.max(logits, axis=0, keepdims=True)
                total = jnp.sum(jnp.exp(logits - highest), axis=0, keepdims=True)
                results.append((logits, jnp.concatenate([highest, total], axis=0)))
            for i, (logits, part) in zip(places, results):
                kept_ref[group * PER_Y + i] = logits
                part_ref[group * PER_Y + by_core(i)] = part

        out(group).start()
    for group in range(NY):
        out(group).wait()


def update_kernel(
    spot_ref, block_ref, low_ref, high_ref, order_ref, many_ref, room_ref,
    rows_ref, cent_ref, logit_ref, norm_ref, out_ref,
    held_ref, kept_ref, sum_ref, mass_ref, done_ref, in_sem, kept_sem, out_sem,
):
    def kept(group):
        windows = pl.ds(group * PER_Y, PER_Y)
        return pltpu.make_async_copy(logit_ref.at[windows], kept_ref.at[windows], kept_sem.at[group])

    for group in range(NY):
        fetch(room_ref, rows_ref, held_ref, in_sem, group, lambda copy: copy.start())
        kept(group).start()

    sum_ref[...] = jnp.zeros_like(sum_ref)
    mass_ref[...] = jnp.zeros_like(mass_ref)

    for group in range(NY):
        fetch(room_ref, rows_ref, held_ref, in_sem, group, lambda copy: copy.wait())
        kept(group).wait()

        @pl.loop(0, (many_ref[group] + ABREAST - 1) // ABREAST)
        def _(step):
            results = []
            for n in range(ABREAST):
                i = order_ref[group * PER_Y + step * ABREAST + n]
                window = group * PER_Y + i
                rows = window_rows(held_ref, spot_ref, group, window)
                place = lax.broadcasted_iota(jnp.int32, kept_ref.shape[1:], 1)
                keep = (place >= low_ref[window]) & (place < high_ref[window])
                norm = norm_ref[group * PER_Y + by_core(i)]
                weights = jnp.where(keep, jnp.exp(kept_ref[window] - norm), 0.0).astype(jnp.bfloat16)
                sums = lax.dot_general(weights, rows, (((1,), (0,)), ((), ())), preferred_element_type=jnp.float32)
                mass = jnp.sum(weights.astype(jnp.float32), axis=1, keepdims=True)
                results.append((block_ref[window], sums, mass))
            for b, sums, mass in results:
                sum_ref[b] += sums
                mass_ref[b] += mass

    def out(b):
        return pltpu.make_async_copy(done_ref.at[b], out_ref.at[b], out_sem.at[b])

    stored = cent_ref.shape[0]
    for b in range(stored):
        new = (sum_ref[b] + prior_mass * cent_ref[b].astype(jnp.float32)) / (mass_ref[b] + prior_mass)
        done_ref[b] = new.astype(done_ref.dtype)
        out(b).start()
    for b in range(stored):
        out(b).wait()


def score(rows, spots, serving, room, centroids):
    stored, lanes, width = centroids.shape
    span = SPAN * GRAIN
    block, _, _, order, many = serving
    smem, vmem = pl.BlockSpec(memory_space=pltpu.SMEM), pl.BlockSpec(memory_space=pltpu.VMEM)
    return pl.pallas_call(
        score_kernel,
        in_specs=[smem] * 5 + [pl.BlockSpec(memory_space=pl.ANY), vmem],
        out_specs=[pl.BlockSpec(memory_space=pl.ANY), vmem],
        out_shape=[
            jax.ShapeDtypeStruct((NDP, lanes, span), jnp.float32),
            jax.ShapeDtypeStruct((NDP, 2, span), jnp.float32),
        ],
        scratch_shapes=[
            pltpu.VMEM(rows.shape, rows.dtype),
            pltpu.VMEM((NDP, lanes, span), jnp.float32),
            pltpu.VMEM((stored, lanes, 1), jnp.float32),
            pltpu.SemaphoreType.DMA((NY, len(PIECES) - 1)),
            pltpu.SemaphoreType.DMA((NY,)),
        ],
        compiler_params=pltpu.CompilerParams(vmem_limit_bytes=VMEM_LIMIT),
        cost_estimate=pl.CostEstimate(
            flops=NDP * lanes * span * width, bytes_accessed=2 * rows.size, transcendentals=NDP * lanes * span
        ),
    )(spots.reshape(-1), block, order, many, room, rows, centroids)


def update(rows, spots, serving, room, centroids, logits, norms):
    stored, lanes, width = centroids.shape
    span = SPAN * GRAIN
    smem, vmem = pl.BlockSpec(memory_space=pltpu.SMEM), pl.BlockSpec(memory_space=pltpu.VMEM)
    hbm = pl.BlockSpec(memory_space=pl.ANY)
    return pl.pallas_call(
        update_kernel,
        in_specs=[smem] * 7 + [hbm, vmem, hbm, vmem],
        out_specs=hbm,
        out_shape=jax.ShapeDtypeStruct(centroids.shape, centroids.dtype),
        scratch_shapes=[
            pltpu.VMEM(rows.shape, rows.dtype),
            pltpu.VMEM((NDP, lanes, span), jnp.float32),
            pltpu.VMEM((stored, lanes, width), jnp.float32),
            pltpu.VMEM((stored, lanes, 1), jnp.float32),
            pltpu.VMEM(centroids.shape, centroids.dtype),
            pltpu.SemaphoreType.DMA((NY, len(PIECES) - 1)),
            pltpu.SemaphoreType.DMA((NY,)),
            pltpu.SemaphoreType.DMA((stored,)),
        ],
        compiler_params=pltpu.CompilerParams(vmem_limit_bytes=VMEM_LIMIT),
        cost_estimate=pl.CostEstimate(
            flops=NDP * lanes * span * width, bytes_accessed=2 * rows.size, transcendentals=NDP * lanes * span
        ),
    )(spots.reshape(-1), *serving, room, rows, centroids, logits, norms)


def joint(former, latter):
    highest = jnp.maximum(former[0:1], latter[0:1])
    total = former[1:2] * jnp.exp(former[0:1] - highest) + latter[1:2] * jnp.exp(latter[0:1] - highest)
    return jnp.concatenate([highest, total], axis=0)


def plane_peers(y, z, c):
    ys = [lax.rem(y + d, NY) for d in range(NY)]
    zs = [lax.rem(z + d, NZ) for d in range(NZ)]
    cs = [lax.rem(c + d, NC) for d in range(NC)]
    far = sorted(range(NZ), key=lambda d: -min(d, NZ - d))
    return [(ys[a], zs[d], cs[b]) for d in far for a in range(NY) for b in range(NC) if a or d or b]


def by_depth(y, z, c):
    return (y * NC + c) * NZ + z


def post(source, target, sent, landed, device):
    pltpu.make_async_remote_copy(source, target, sent, landed, device_id=device, device_id_type=MESH).start()


def await_all(buffer, count, sent, landed):
    piece = buffer.at[pl.ds(0, count)]
    pltpu.make_async_copy(piece, piece, sent).wait()
    pltpu.make_async_copy(piece, piece, landed).wait()


def census_kernel(count_ref, all_ref, land_ref, sems):
    y, z, c, q = (lax.axis_index(a) for a in ("y", "z", "core", "cand"))
    here = (y * NZ + z) * NC + c
    peers = plane_peers(y, z, c)
    barrier = pltpu.get_barrier_semaphore()
    for peer in peers:
        pl.semaphore_signal(barrier, 1, device_id=peer + (q,), device_id_type=MESH)
    pl.semaphore_wait(barrier, len(peers))
    for peer in peers:
        post(count_ref, land_ref.at[here], sems.at[0], sems.at[1], peer + (q,))
    land_ref[here] = count_ref[...]
    await_all(land_ref, len(peers), sems.at[0], sems.at[1])
    all_ref[...] = land_ref[...]


def census(counts, collective_id):
    lanes = 128
    vmem = pl.BlockSpec(memory_space=pltpu.VMEM)
    shape = (NDP, 1, lanes)
    every = pl.pallas_call(
        census_kernel,
        in_specs=[vmem],
        out_specs=vmem,
        out_shape=jax.ShapeDtypeStruct(shape, counts.dtype),
        scratch_shapes=[pltpu.VMEM(shape, counts.dtype), pltpu.SemaphoreType.DMA((2,))],
        compiler_params=pltpu.CompilerParams(
            collective_id=collective_id, has_side_effects=True, vmem_limit_bytes=16 * 2**20
        ),
    )(jnp.pad(counts, (0, lanes - counts.size))[None])
    return every[:, 0, : counts.size]


def exchange_kernel(
    first_ref, second_ref, pick_ref, begin_ref, low_ref, high_ref, part_ref, got_ref, log_ref,
    back_ref, half_ref, quarters_ref, own_ref, send_ref, land_ref, sems,
):
    y, z, c, q = (lax.axis_index(a) for a in ("y", "z", "core", "cand"))
    listed = own_ref.shape[0]
    peers = plane_peers(y, z, c)
    here = by_depth(y, z, c)
    mates = [(y, z, c, lax.rem(q + d, NQ)) for d in range(1, NQ)]
    barrier = pltpu.get_barrier_semaphore()
    for peer in peers:
        pl.semaphore_signal(barrier, 1, device_id=peer + (q,), device_id_type=MESH)
    for mate in mates:
        pl.semaphore_signal(barrier, 1, device_id=mate, device_id_type=MESH)
    pl.semaphore_wait(barrier, len(peers) + len(mates))

    def send(source, target, kind, device):
        post(source, target, sems.at[kind, 0], sems.at[kind, 1], device)

    def settle(buffer, count, kind):
        await_all(buffer, count, sems.at[kind, 0], sems.at[kind, 1])

    for peer in peers:
        send(part_ref.at[by_depth(*peer)], back_ref.at[here], 0, peer + (q,))
    back_ref[here] = part_ref[here]
    settle(back_ref, len(peers), 0)

    for e in range(listed):
        half_ref[e] = joint(back_ref[first_ref[e]], back_ref[second_ref[e]])
    for n, mate in enumerate(mates):
        send(half_ref, quarters_ref.at[n], 1, mate)
    settle(quarters_ref, len(mates), 1)
    for e in range(listed):
        both = joint(half_ref[e], quarters_ref[0, e])
        rest = joint(quarters_ref[1, e], quarters_ref[2, e])
        pair = joint(both, rest)
        own_ref[e] = pair[0:1] + jnp.log(pair[1:2])

    for peer in peers:
        index = by_depth(*peer)
        send_ref[index] = own_ref[pick_ref[index]]
        send(send_ref.at[index], land_ref.at[here], 2, peer + (q,))
    land_ref[here] = own_ref[pick_ref[here]]

    grain = lax.broadcasted_iota(jnp.int32, (log_ref.shape[0], SPAN * GRAIN), 0)
    row = lax.broadcasted_iota(jnp.int32, (log_ref.shape[0], SPAN * GRAIN), 1)
    spread = jnp.zeros(grain.shape, jnp.float32)
    for e in range(listed):
        keep = (row >= low_ref[e]) & (row < high_ref[e]) & (grain - begin_ref[e] == row // GRAIN)
        spread += jnp.where(keep, own_ref[e], 0.0)
    row = lax.broadcasted_iota(jnp.int32, (SPAN * GRAIN, GRAIN), 0)
    column = lax.broadcasted_iota(jnp.int32, (SPAN * GRAIN, GRAIN), 1)
    fold = (row % GRAIN == column).astype(jnp.float32)
    log_ref[...] = jnp.dot(spread, fold, precision=lax.Precision.HIGHEST, preferred_element_type=jnp.float32)

    settle(land_ref, len(peers), 2)
    got_ref[...] = land_ref[...]


def exchange(first, second, pick, begin, low, high, part, grains, collective_id):
    listed = first.shape[0]
    span = SPAN * GRAIN
    smem, vmem = pl.BlockSpec(memory_space=pltpu.SMEM), pl.BlockSpec(memory_space=pltpu.VMEM)
    buffer = lambda *shape: pltpu.VMEM(shape + (span,), jnp.float32)
    return pl.pallas_call(
        exchange_kernel,
        in_specs=[smem] * 6 + [vmem],
        out_specs=[vmem, vmem],
        out_shape=[
            jax.ShapeDtypeStruct((NDP, 1, span), jnp.float32),
            jax.ShapeDtypeStruct((grains, GRAIN), jnp.float32),
        ],
        scratch_shapes=[
            buffer(NDP, 2), buffer(listed, 2), buffer(NQ - 1, listed, 2), buffer(listed, 1), buffer(NDP, 1), buffer(NDP, 1),
            pltpu.SemaphoreType.DMA((3, 2)),
        ],
        compiler_params=pltpu.CompilerParams(
            collective_id=collective_id, has_side_effects=True, vmem_limit_bytes=16 * 2**20
        ),
    )(first, second, pick, begin, low, high, part)


def on_device(embeddings, point_parent, parent_list, block_slots, centroids):
    y, z, c, q = (lax.axis_index(a) for a in ("y", "z", "core", "cand"))
    here = (y * NZ + z) * NC + c
    row_count, width = embeddings.shape
    stored = centroids.shape[0]
    listed = parent_list.shape[1]
    grains = row_count // GRAIN
    local = grains // NQ
    i32 = jnp.int32

    share = lax.dynamic_index_in_dim(embeddings.reshape(local, NQ, GRAIN, width), q, 1, keepdims=False)
    shares = lax.all_gather(share, ("z", "core"), axis=0, tiled=True)

    counts = jnp.sum((point_parent[:, None] == parent_list[here][None, :]).astype(i32), axis=0)
    counts = census(counts, 2)
    starts = jnp.cumsum(counts, axis=1) - counts
    begin = starts // GRAIN
    last = (starts + counts - 1) // GRAIN
    low = starts % GRAIN
    high = low + counts
    slots = jnp.take(block_slots, parent_list, axis=0)
    owner = slots // (stored * NQ)
    planes = jnp.arange(NQ, dtype=i32)

    def share_of(begin, last, plane):
        nearest = begin + (plane - begin) % NQ
        return nearest, (nearest <= last).astype(i32) + (nearest + NQ <= last).astype(i32)

    loads = share_of(begin[..., None], last[..., None], planes)[1]
    loads = jnp.broadcast_to(loads[:, :, None, :], (NDP, listed, 2, NQ)).reshape(NY, PER_Y * listed * 2, NQ)
    takers = jnp.swapaxes(owner, 2, 3).reshape(NY, PER_Y * listed * 2, NQ)
    takes = takers[..., None] == jnp.arange(NDP, dtype=i32)
    totals = jnp.einsum(
        "ymqj,ymp->yqjp", takes.astype(jnp.bfloat16), loads.astype(jnp.bfloat16), preferred_element_type=jnp.float32
    )
    size = jnp.sum((jnp.max(totals) > jnp.asarray(ROOMS[:-1], jnp.float32)).astype(i32))
    room = jnp.asarray(ROOMS, i32)[size][None]

    mine = jnp.take(owner, q, axis=2) == here
    entry = jnp.any(mine, axis=2)
    chosen = lambda value: jnp.sum(jnp.where(entry, value, 0), axis=1)
    served = jnp.any(entry, axis=1)
    serve_low, serve_high, serve_begin = chosen(low), chosen(high), chosen(begin)
    serve_last = jnp.where(served, chosen(last), -1)
    serve_block = jnp.sum(jnp.where(mine, jnp.take(slots, q, axis=2) % stored, 0), axis=(1, 2))
    grouped = served.reshape(NY, PER_Y).astype(i32)
    many = jnp.sum(grouped, axis=1)
    rank = jnp.where(
        grouped > 0, jnp.cumsum(grouped, axis=1) - 1, many[:, None] + jnp.cumsum(1 - grouped, axis=1) - 1
    )
    around = jnp.arange(PER_Y, dtype=i32)
    order = jnp.sum(jnp.where(rank[:, :, None] == around, around[None, :, None], 0), axis=1).reshape(-1)
    serving = (serve_block, serve_low, serve_high, order, many)

    _, landing = share_of(serve_begin[:, None], serve_last[:, None], planes)
    landing = landing.reshape(NY, PER_Y, NQ)
    base = (jnp.cumsum(landing, axis=1) - landing).reshape(NDP, NQ)
    step = jnp.arange(SPAN, dtype=i32)
    grain = serve_begin[:, None] + step
    plane = grain % NQ
    within = jnp.sum(jnp.where(plane[..., None] == planes, base[:, None, :], 0), axis=2) + step // NQ
    real = grain <= serve_last[:, None]
    within = jnp.where(real, within, within[:, :1])
    plane = jnp.where(real, plane, plane[:, :1])
    within = jnp.where(served[:, None], within, 0)

    own = lambda value: lax.dynamic_index_in_dim(value, here, 0, keepdims=False)
    dps = jnp.arange(NDP, dtype=i32)
    depth_order = dps.reshape(NY, NZ, NC).transpose(0, 2, 1).reshape(-1)
    own_owner = own(jnp.take(owner, q, axis=2))
    pick = jnp.sum(
        jnp.where(own_owner[None] == depth_order[:, None, None], jnp.arange(listed, dtype=i32)[None, :, None], 0),
        axis=(1, 2),
    )
    deep = lambda index: by_depth(index // PER_Y, index // NC % NZ, index % NC)

    of_y = lambda value: lax.dynamic_index_in_dim(value.reshape((NY, PER_Y) + value.shape[1:]), y, 0, keepdims=False)
    target = (jnp.arange(NY, dtype=i32) * NZ + z) * NC + c
    hit = jnp.any(of_y(owner)[None] == target[:, None, None, None, None], axis=-1)
    sent = lambda value: jnp.sum(jnp.where(hit, of_y(value)[None, :, :, None], 0), axis=2)
    nearest, sending = share_of(sent(begin), jnp.where(jnp.any(hit, axis=2), sent(last), -1), q)
    place = jnp.cumsum(sending, axis=1) - sending
    places = jnp.arange(FULL, dtype=i32)
    picks = 0
    for slot in range(2):
        here_now = (place[..., None] + slot == places) & (sending[..., None] > slot)
        which = around[:, None] * local + nearest // NQ + slot
        picks = picks + jnp.sum(jnp.where(here_now, which[..., None], 0), axis=1)
    picks = picks.reshape(NY * NQ, FULL)

    branches = [functools.partial(dispatch, most, 3 + n) for n, most in enumerate(ROOMS)]
    rows = lax.switch(size, branches, shares, picks)
    rows = rows.reshape(NY, NQ, FULL, GRAIN, width)
    spots = plane * FULL + within
    logits, part = score(rows, spots, serving, room, centroids)
    norms, log_norms = exchange(
        deep(own_owner[:, 0]), deep(own_owner[:, 1]), pick, own(begin), own(low), own(high), part, grains, 1
    )
    updated = update(rows, spots, serving, room, centroids, logits, norms)
    return updated, log_norms.reshape(row_count)


def solution(mesh):
    split = Mesh(mesh.devices.reshape(NY, NZ, NC, NQ), ("y", "z", "core", "cand"))
    dp = ("y", "z", "core")
    every = dp + ("cand",)
    return jax.shard_map(
        on_device,
        mesh=split,
        in_specs=(P(dp, None), P(dp), P(), P(), P(every, None, None)),
        out_specs=(P(every, None, None), P(dp)),
        check_vma=False,
    )
```

time: 253 us -> 241 us (0.953)
  blocking collectives: 21.2 us -> 0 us
  waiting for transfers between devices: 2.63 us -> 10.3 us
  Pallas kernels: 167 us -> 173 us
  other arithmetic: 15.3 us -> 11.6 us
    unnamed x1 -> x0, blocking collectives: 21.2 us -> none
    all_gather x1, waiting for transfers between devices: 2.62 us -> 10.2 us  [on_device(): shares = lax.all_gather(share, ('z', 'core'), axis=0, tiled=True)]
    pallas_call x3 -> x4, Pallas kernels: 54.5 us -> 61.6 us  [the longest x1 21.5 us: exchange(): pl.pallas_call(exchange_kernel, in_specs=[smem] * 6 + [vmem], out_specs=[...]
    unnamed x21 -> x14, local copies, waits for them, and re-layouts: 6.16 us -> 4.63 us
  transfers between devices with their start and end apart: 1 -> 1, of which waited for: 1 -> 1; matrix products, arithmetic and copies ran while one was open for 14% -> 13% of each run, Pallas kernels for 0% -> 6%
where the time goes in v3:
time: 241 us; the launch traced here: 240 us
  Pallas kernels  173 us (72%)
  local copies, waits for them, and re-layouts  26.5 us (11%)
  between operations  17 us (7%)
  other arithmetic  11.6 us (5%)
  waiting for transfers between devices  10.3 us (4%)
    pallas_call x1, Pallas kernels, dispatch(): pl.pallas_call(functools.partial(dispatch_kernel, room), in_specs=[pl.Blo...  111 us
    pallas_call x1, Pallas kernels, exchange(): pl.pallas_call(exchange_kernel, in_specs=[smem] * 6 + [vmem], out_specs=[...  21.5 us
    pallas_call x1, Pallas kernels, census(): pl.pallas_call(census_kernel, in_specs=[vmem], out_specs=vmem, out_shape=...  15.2 us
    pallas_call x1, Pallas kernels, update(): pl.pallas_call(update_kernel, in_specs=[smem] * 7 + [hbm, vmem, hbm, vmem...  13.2 us
    pallas_call x1, Pallas kernels, score(): pl.pallas_call(score_kernel, in_specs=[smem] * 5 + [pl.BlockSpec(memory_s...  11.7 us
    all_gather x1, waiting for transfers between devices, on_device(): shares = lax.all_gather(share, ('z', 'core'), axis=0, tiled=True)  10.2 us
    gather x3, local copies, waits for them, and re-layouts, on_device(): slots = jnp.take(block_slots, parent_list, axis=0)  6.46 us
  transfers between devices with their start and end apart: 1, of which 1 were waited for; matrix products, arithmetic and copies ran while one was open for 13% of the time, Pallas kernels for 6%

profile of v3, /device:TPU:1, one launch (start us, length us, event | category | flops | bytes accessed | tf_op | source)
XLA Modules:
  0.0 240.4 jit_solution(9944472345656909323)
XLA Ops:
  7.2 1.5 copy-done
  8.8 0.8 constant_dynamic-slice_fusion.4
  9.6 0.8 copy.232
  10.4 0.9 dynamic-slice_reduce_fusion
  11.3 0.9 convert_reduce_fusion
  12.2 15.2 %shard_map.86 = s32[64,1,128]{2,1,0:T(1,128)S(1)} custom-call(s32[1,128]{1,0:T(1,128)S(1)} %pad_bitcast_fusion.count_ref), custom_call_target="tpu_custom_call" | custom-call | tf_op jit(solution)/shard_map/pallas_call | solution.py:310
  27.4 0.2 reduce_window_sum.49
  27.7 0.9 copy.235
  28.6 3.6 %gather_fusion = s32[1024,4,2]{1,2,0:T(2,128)S(1)} fusion(s32[256,4,2]{1,2,0:T(2,128)S(1)} %copy.235, s32[1024]{0:T(1024)S(1)} %broadcast_clamp_fusion), kind=kCustom, calls=%fused_computation | custom fusion | bytes 69632 | tf_op jit(solution)/shard_map/jit(_take)/gather | solution.py:425
  32.1 1.8 copy.289
  33.9 1.8 add_select_fusion.1
  35.7 2.6 %copy.240 = s32[64,16,2,4]{3,2,1,0:T(2,128)} copy(s32[64,16,2,4]{1,0,2,3:T(8,128)} %get-tuple-element.1062) | data formatting | bytes 65536 | tf_op jit(solution)/shard_map/jit(floor_divide)/jit(_where)/select_n | solution.py:426
  38.3 2.2 copy.241
  40.5 1.3 fusion.21
  42.0 1.3 select_reduce_fusion.20
  43.3 0.5 add_convert_fusion
  43.9 0.3 broadcast_in_dim.341
  44.2 1.9 fusion.2
  46.1 1.3 fusion.58
  48.7 1.1 copy.243
  50.1 0.4 compare_reduce_fusion.1
  50.6 0.6 select_reduce_fusion.17
  51.2 0.2 copy.246
  51.4 0.2 copy.245
  51.6 0.2 reduce_window_sum.52
  52.0 0.2 reduce_window_sum.53
  52.3 0.7 reshape.550.order_ref
  55.9 0.6 dynamic_slice.36.room_ref
  56.5 0.7 fusion.63.high_ref
  57.2 0.7 constant_dynamic-slice_fusion.3
  57.9 0.7 fusion.61
  58.6 0.2 select_reduce_fusion.18.pick_ref
  58.8 0.6 fusion.53.spot_ref
  59.4 0.3 fusion.14
  59.8 10.2 %all-gather.3.cloned.1.call-done = bf16[256,1,16,1024]{3,2,1,0:T(8,128)(2,1)} async-done(((bf16[16,1,16,1024]{3,2,1,0:T(8,128)(2,1)}), bf16[256,1,16,1024]{3,2,1,0:T(8,128)(2,1)}) %all-gather.3.cloned.1.call-update) | async-done | bytes 8388624 | tf_op jit(solution)/shard_map/all_gather | solution.py:416
  70.1 114.9 %conditional.1 = (bf16[4,4,32,16,1024]{4,3,2,1,0:T(8,128)(2,1)}) conditional(s32[]{:T(128)} %clamp.3, (s32[4,16,4,1]{3,2,1,0:T(4,128)S(1)}, s32[4,16,4,32]{3,2,1,0:T(4,128)S(1)}, s32[4,16,4,1]{3,2,1,0:T(4,128)S(1)}, s32[4,16,4,1]{3,2,1,0:T(4,128)S(1)}, s32[4,16,4,1]{3,2,1,0:T(4,128)S(1)}, ...), branch_computations={%region_22.26_spmd, %region_25.29_spmd, %region_28.32_spmd, %regio... | conditional | flops 66048 | bytes 25305096 | solution.py:496
  70.6 0.5 copy.261
  71.2 0.5 copy.260
  71.7 0.5 copy.259
  72.2 0.6 select_reduce_fusion.4
  72.8 0.7 add.480.pick_ref
  73.5 111.4 %branch_2_fun.2 = bf16[16,32,16,1024]{3,2,1,0:T(8,128)(2,1)} custom-call(s32[512]{0:T(512)} %add.480.pick_ref, bf16[256,16,1024]{2,1,0:T(8,128)(2,1)} %get-tuple-element.677.share_ref), custom_call_target="tpu_custom_call" | custom-call | bytes 17825792 | tf_op jit(solution)/shard_map/cond/branch_2_fun/pallas_call | solution.py:73
  185.0 11.7 %shard_map.87 = (f32[64,128,128]{2,1,0:T(8,128)}, f32[64,2,128]{2,1,0:T(2,128)}) custom-call(s32[512]{0:T(512)} %fusion.53.spot_ref, s32[64]{0:T(128)} %get-tuple-element.1064.block_ref, s32[64]{0:T(128)} %reshape.550.order_ref, s32[4]{0:T(128)} %copy-done.3, s32[1]{0:T(128)} %dynamic_slice.36.room_ref, ...), custom_call_target="tpu_custom_call" | custom-call | flops 1073741824 | bytes 16777216 | tf_op jit(solution)/shard_map/pallas_call | solution.py:214
  196.8 0.8 copy-done.1
  197.6 21.5 %shard_map.88 = (f32[64,1,128]{2,1,0:T(1,128)S(1)}, f32[64,16]{1,0:T(8,128)S(1)}) custom-call(s32[16]{0:T(128)S(1)} %get-tuple-element.1096.first_ref, s32[16]{0:T(128)S(1)} %get-tuple-element.1095.second_ref, s32[64]{0:T(128)S(1)} %select_reduce_fusion.18.pick_ref, s32[16]{0:T(128)S(1)} %get-tuple-element.1101.begin_ref, ...), custom_call_target="tpu_custom_call" | custom-call | tf_op jit(solution)/shard_map/pallas_call | solution.py:387
  219.1 0.6 copy-done.2
  219.7 0.7 reshape.559
  220.4 13.2 %shard_map.89 = bf16[8,128,1024]{2,1,0:T(8,128)(2,1)} custom-call(s32[512]{0:T(512)} %fusion.53.spot_ref, s32[64]{0:T(128)} %get-tuple-element.1064.block_ref, s32[64]{0:T(128)} %get-tuple-element.1055.low_ref, s32[64]{0:T(128)} %get-tuple-element.1054.high_ref, s32[64]{0:T(128)} %reshape.550.order_ref, s32[4]{0:T(128)} %copy-done.3, ...), custom_call_target="tpu_custom_call" | custom-call | flops 1073741824 | bytes 16777216 | tf_op jit(solution)/shard_map/pallas_call | solution.py:241
  (75 shorter events, 3.3 us)
Async XLA Ops:
  7.2 1.6 copy-start
  7.2 38.9 %copy-start.5 = (f32[7]{0:T(128)S(1)}, f32[7]{0:T(128)}, u32[]{:S(2)}) copy-start(f32[7]{0:T(128)} %constant.319.clone) | copy-start | bytes 88
  7.2 62.8 %all-gather.3.cloned.1.call-start = ((), (), s32[]{:S(2)}) async-start(), calls=%async_computation | async-start | bytes 8912896 | tf_op jit(solution)/shard_map/all_gather | solution.py:416
  27.7 28.2 %copy-start.4 = (s32[8]{0:T(128)S(1)}, s32[8]{0:T(128)}, u32[]{:S(2)}) copy-start(s32[8]{0:T(128)} %constant.320.clone) | copy-start | bytes 100
  52.0 18.2 %copy-start.3 = (s32[4]{0:T(128)}, s32[4]{0:T(128)S(1)}, u32[]{:S(2)}) copy-start(s32[4]{0:T(128)S(1)} %get-tuple-element.1093.many_ref) | copy-start | bytes 52
  196.8 0.8 copy-start.1
  219.1 0.6 copy-start.2
Sparse Core Ops, SparseCore 0:
  9.9 60.1 all-gather.2

commit v4 on v3

v4 whole, which is shorter than its diff:
```python
import functools

import jax
import jax.numpy as jnp
from jax import lax
from jax.experimental import pallas as pl
from jax.experimental.pallas import tpu as pltpu
from jax.sharding import Mesh
from jax.sharding import PartitionSpec as P

sharpness = 3.0
prior_mass = 1.0

GRAIN = 16
SPAN = 8
NY, NZ, NC, NQ = 4, 8, 2, 4
NDP = NY * NZ * NC
PER_Y = NZ * NC
ABREAST = 4
FULL = 2 * PER_Y
ROOMS = (17, 19, 22, FULL)
STEPS = (
    ((1, 1), (3, 3), (1, 3), (3, 1), (1, 0), (3, 0), (1, 2), (3, 2)),
    ((0, 1), (0, 3), (2, 1), (2, 3), (2, 2), (0, 2), (2, 0)),
)
MESH = pl.DeviceIdType.MESH
VMEM_LIMIT = 56 * 2**20


def by_core(i):
    return (i % NC) * NZ + i // NC


def fetch(room, rows_ref, held_ref, sems, group):
    places = pl.ds(0, room)
    return pltpu.make_async_copy(rows_ref.at[group, :, places], held_ref.at[group], sems.at[group])


def window_rows(held_ref, spot_ref, group, window):
    spots = [spot_ref[window * SPAN + k] for k in range(SPAN)]
    return jnp.concatenate([held_ref[group, spot // FULL, spot % FULL] for spot in spots], axis=0)


def update_kernel(
    room, spot_ref, block_ref, low_ref, high_ref, order_ref, many_ref,
    rows_ref, cent_ref, logit_ref, norm_ref, out_ref,
    held_ref, kept_ref, sum_ref, mass_ref, done_ref, in_sem, kept_sem, out_sem,
):
    def kept(group):
        windows = pl.ds(group * PER_Y, PER_Y)
        return pltpu.make_async_copy(logit_ref.at[windows], kept_ref.at[windows], kept_sem.at[group])

    for group in range(NY):
        fetch(room, rows_ref, held_ref, in_sem, group).start()
        kept(group).start()

    sum_ref[...] = jnp.zeros_like(sum_ref)
    mass_ref[...] = jnp.zeros_like(mass_ref)

    @pl.loop(0, NY)
    def _(group):
        fetch(room, rows_ref, held_ref, in_sem, group).wait()
        kept(group).wait()

        @pl.loop(0, (many_ref[group] + ABREAST - 1) // ABREAST)
        def _(step):
            results = []
            for n in range(ABREAST):
                i = order_ref[group * PER_Y + step * ABREAST + n]
                window = group * PER_Y + i
                rows = window_rows(held_ref, spot_ref, group, window)
                place = lax.broadcasted_iota(jnp.int32, kept_ref.shape[1:], 1)
                keep = (place >= low_ref[window]) & (place < high_ref[window])
                norm = norm_ref[group * PER_Y + by_core(i)]
                weights = jnp.where(keep, jnp.exp(kept_ref[window] - norm), 0.0).astype(jnp.bfloat16)
                sums = lax.dot_general(weights, rows, (((1,), (0,)), ((), ())), preferred_element_type=jnp.float32)
                mass = jnp.sum(weights.astype(jnp.float32), axis=1, keepdims=True)
                results.append((block_ref[window], sums, mass))
            for b, sums, mass in results:
                sum_ref[b] += sums
                mass_ref[b] += mass

    def out(b):
        return pltpu.make_async_copy(done_ref.at[b], out_ref.at[b], out_sem.at[b])

    stored = cent_ref.shape[0]

    @pl.loop(0, stored)
    def _(b):
        new = (sum_ref[b] + prior_mass * cent_ref[b].astype(jnp.float32)) / (mass_ref[b] + prior_mass)
        done_ref[b] = new.astype(done_ref.dtype)
        out(b).start()
    @pl.loop(0, stored)
    def _(b):
        out(b).wait()


def update(rows, spots, serving, room, centroids, logits, norms):
    stored, lanes, width = centroids.shape
    span = SPAN * GRAIN
    smem, vmem = pl.BlockSpec(memory_space=pltpu.SMEM), pl.BlockSpec(memory_space=pltpu.VMEM)
    hbm = pl.BlockSpec(memory_space=pl.ANY)
    return pl.pallas_call(
        functools.partial(update_kernel, room),
        in_specs=[smem] * 6 + [hbm, vmem, hbm, vmem],
        out_specs=hbm,
        out_shape=jax.ShapeDtypeStruct(centroids.shape, centroids.dtype),
        scratch_shapes=[
            pltpu.VMEM((NY, NQ, room) + rows.shape[3:], rows.dtype),
            pltpu.VMEM((NDP, lanes, span), jnp.float32),
            pltpu.VMEM((stored, lanes, width), jnp.float32),
            pltpu.VMEM((stored, lanes, 1), jnp.float32),
            pltpu.VMEM(centroids.shape, centroids.dtype),
            pltpu.SemaphoreType.DMA((NY,)),
            pltpu.SemaphoreType.DMA((NY,)),
            pltpu.SemaphoreType.DMA((stored,)),
        ],
        compiler_params=pltpu.CompilerParams(vmem_limit_bytes=VMEM_LIMIT),
        cost_estimate=pl.CostEstimate(
            flops=NDP * lanes * span * width, bytes_accessed=2 * rows.size, transcendentals=NDP * lanes * span
        ),
    )(spots, *serving, rows, centroids, logits, norms)


def joint(former, latter):
    highest = jnp.maximum(former[0:1], latter[0:1])
    total = former[1:2] * jnp.exp(former[0:1] - highest) + latter[1:2] * jnp.exp(latter[0:1] - highest)
    return jnp.concatenate([highest, total], axis=0)


def plane_peers(y, z, c):
    ys = [lax.rem(y + d, NY) for d in range(NY)]
    zs = [lax.rem(z + d, NZ) for d in range(NZ)]
    cs = [lax.rem(c + d, NC) for d in range(NC)]
    far = sorted(range(NZ), key=lambda d: -min(d, NZ - d))
    return [(ys[a], zs[d], cs[b]) for d in far for a in range(NY) for b in range(NC) if a or d or b]


def by_depth(y, z, c):
    return (y * NC + c) * NZ + z


def post(source, target, sent, landed, device):
    pltpu.make_async_remote_copy(source, target, sent, landed, device_id=device, device_id_type=MESH).start()


def await_all(buffer, count, sent, landed):
    piece = buffer.at[pl.ds(0, count)]
    pltpu.make_async_copy(piece, piece, sent).wait()
    pltpu.make_async_copy(piece, piece, landed).wait()


def census_kernel(count_ref, all_ref, land_ref, sems):
    y, z, c, q = (lax.axis_index(a) for a in ("y", "z", "core", "cand"))
    here = (y * NZ + z) * NC + c
    peers = plane_peers(y, z, c)
    barrier = pltpu.get_barrier_semaphore()
    for peer in peers:
        pl.semaphore_signal(barrier, 1, device_id=peer + (q,), device_id_type=MESH)
    pl.semaphore_wait(barrier, len(peers))
    for peer in peers:
        post(count_ref, land_ref.at[here], sems.at[0], sems.at[1], peer + (q,))
    land_ref[here] = count_ref[...]
    await_all(land_ref, len(peers), sems.at[0], sems.at[1])
    all_ref[...] = land_ref[...]


def census(counts, collective_id):
    lanes = 128
    vmem = pl.BlockSpec(memory_space=pltpu.VMEM)
    shape = (NDP, 1, lanes)
    every = pl.pallas_call(
        census_kernel,
        in_specs=[vmem],
        out_specs=vmem,
        out_shape=jax.ShapeDtypeStruct(shape, counts.dtype),
        scratch_shapes=[pltpu.VMEM(shape, counts.dtype), pltpu.SemaphoreType.DMA((2,))],
        compiler_params=pltpu.CompilerParams(
            collective_id=collective_id, has_side_effects=True, vmem_limit_bytes=16 * 2**20
        ),
    )(jnp.pad(counts, (0, lanes - counts.size))[None])
    return every[:, 0, : counts.size]


def serve_kernel(
    room, pick_ref, spot_ref, block_ref, first_ref, second_ref, entry_ref, begin_ref, low_ref, high_ref,
    share_ref, cent_ref, rows_ref, logit_ref, got_ref, log_ref,
    grains_ref, send_ref, held_refs, kept_ref, square_ref, part_ref,
    back_ref, half_ref, quarters_ref, own_ref, fore_ref, land_ref,
    load_sem, send_sem, recv_sem, out_sem, sems,
):
    y, z, c, q = (lax.axis_index(a) for a in ("y", "z", "core", "cand"))
    here = y * NQ + q
    deep = by_depth(y, z, c)
    peers = plane_peers(y, z, c)
    mates = [(y, z, c, lax.rem(q + d, NQ)) for d in range(1, NQ)]

    def target(step):
        ty, tq = lax.rem(y + step[0], NY), lax.rem(q + step[1], NQ)
        return ty * NQ + tq, (ty, z, c, tq)

    load = pltpu.make_async_copy(share_ref, grains_ref, load_sem.at[0])
    load.start()
    slanted = [target(step)[1] for phase in STEPS for step in phase if step[0] and step[1]]
    barrier = pltpu.get_barrier_semaphore()
    for device in [peer + (q,) for peer in peers] + mates + slanted:
        pl.semaphore_signal(barrier, 1, device_id=device, device_id_type=MESH)
    pl.semaphore_wait(barrier, len(peers) + len(mates) + len(slanted))
    load.wait()

    def lands(phase, step):
        return held_refs[phase].at[((NY - step[0]) % NY) // 2 * NQ + q]

    def copy(phase, n, places):
        step = STEPS[phase][n]
        index, device = target(step)
        return pltpu.make_async_remote_copy(
            send_ref.at[index, places], lands(phase, step).at[places], send_sem.at[phase, n], recv_sem.at[phase, n],
            device_id=device, device_id_type=MESH,
        )

    for phase, steps in enumerate(STEPS):

        @pl.loop(0, room)
        def _(place):
            for n, step in enumerate(steps):
                index, _ = target(step)
                send_ref[index, place] = grains_ref[pick_ref[index * FULL + place]]
                copy(phase, n, pl.ds(place, 1)).start()
            if phase == 1:
                send_ref[here, place] = grains_ref[pick_ref[here * FULL + place]]

    kept = pltpu.make_async_copy(send_ref.at[here], lands(1, (0, 0)), load_sem.at[1])
    kept.start()

    @pl.loop(0, cent_ref.shape[0])
    def _(b):
        wide = cent_ref[b].astype(jnp.float32)
        square_ref[b] = jnp.sum(wide * wide, axis=1, keepdims=True)

    def group_of(phase, side):
        return lax.rem(y + 2 * side + 1 - phase, NY)

    def rows_out(phase, side):
        return pltpu.make_async_copy(
            held_refs[phase].at[pl.ds(side * NQ, NQ)],
            rows_ref.at[pl.ds(group_of(phase, side) * NQ, NQ), pl.ds(0, room)],
            out_sem.at[phase, side, 0],
        )

    def logits_out(phase, side):
        windows = pl.ds(group_of(phase, side) * PER_Y, PER_Y)
        return pltpu.make_async_copy(kept_ref.at[windows], logit_ref.at[windows], out_sem.at[phase, side, 1])

    for phase, steps in enumerate(STEPS):
        held_ref = held_refs[phase]
        for n in range(len(steps)):
            copy(phase, n, pl.ds(0, room)).wait()
        if phase == 1:
            kept.wait()
        turns = PER_Y // ABREAST

        for side in range(2):
            rows_out(phase, side).start()

        @pl.loop(0, 2 * turns)
        def _(turn):
            side = turn // turns
            group = group_of(phase, side)
            places = [turn % turns * ABREAST + n for n in range(ABREAST)]
            results = []
            for i in places:
                window = group * PER_Y + i
                spots = [spot_ref[window * SPAN + k] for k in range(SPAN)]
                rows = jnp.concatenate([held_ref[side * NQ + spot // FULL, spot % FULL] for spot in spots], axis=0)
                b = block_ref[window]
                scores = lax.dot_general(
                    cent_ref[b], rows, (((1,), (1,)), ((), ())), preferred_element_type=jnp.float32
                )
                logits = sharpness * (scores - 0.5 * square_ref[b])
                highest = jnp.max(logits, axis=0, keepdims=True)
                total = jnp.sum(jnp.exp(logits - highest), axis=0, keepdims=True)
                results.append((logits, jnp.concatenate([highest, total], axis=0)))
            for i, (logits, part) in zip(places, results):
                kept_ref[group * PER_Y + i] = logits
                part_ref[group * PER_Y + by_core(i)] = part

        for side in range(2):
            logits_out(phase, side).start()

    def settle(buffer, count, kind):
        await_all(buffer, count, sems.at[kind, 0], sems.at[kind, 1])

    for peer in peers:
        post(part_ref.at[by_depth(*peer)], back_ref.at[deep], sems.at[0, 0], sems.at[0, 1], peer + (q,))
    back_ref[deep] = part_ref[deep]
    settle(back_ref, len(peers), 0)

    listed = own_ref.shape[0]
    for e in range(listed):
        half_ref[e] = joint(back_ref[first_ref[e]], back_ref[second_ref[e]])
    for n, mate in enumerate(mates):
        post(half_ref, quarters_ref.at[n], sems.at[1, 0], sems.at[1, 1], mate)
    settle(quarters_ref, len(mates), 1)
    for e in range(listed):
        both = joint(half_ref[e], quarters_ref[0, e])
        rest = joint(quarters_ref[1, e], quarters_ref[2, e])
        pair = joint(both, rest)
        own_ref[e] = pair[0:1] + jnp.log(pair[1:2])

    for peer in peers:
        index = by_depth(*peer)
        fore_ref[index] = own_ref[entry_ref[index]]
        post(fore_ref.at[index], land_ref.at[deep], sems.at[2, 0], sems.at[2, 1], peer + (q,))
    land_ref[deep] = own_ref[entry_ref[deep]]

    grain = lax.broadcasted_iota(jnp.int32, (log_ref.shape[0], SPAN * GRAIN), 0)
    row = lax.broadcasted_iota(jnp.int32, (log_ref.shape[0], SPAN * GRAIN), 1)
    spread = jnp.zeros(grain.shape, jnp.float32)
    for e in range(listed):
        keep = (row >= low_ref[e]) & (row < high_ref[e]) & (grain - begin_ref[e] == row // GRAIN)
        spread += jnp.where(keep, own_ref[e], 0.0)
    row = lax.broadcasted_iota(jnp.int32, (SPAN * GRAIN, GRAIN), 0)
    column = lax.broadcasted_iota(jnp.int32, (SPAN * GRAIN, GRAIN), 1)
    fold = (row % GRAIN == column).astype(jnp.float32)
    log_ref[...] = jnp.dot(spread, fold, precision=lax.Precision.HIGHEST, preferred_element_type=jnp.float32)

    settle(land_ref, len(peers), 2)
    got_ref[...] = land_ref[...]
    for phase in range(2):
        for side in range(2):
            rows_out(phase, side).wait()
            logits_out(phase, side).wait()


def serve(room, collective_id, grains, shares, centroids, *tables):
    stored, lanes, width = centroids.shape
    span = SPAN * GRAIN
    targets = NY * NQ
    listed = tables[3].shape[0]
    shape, dtype = shares.shape[1:], shares.dtype
    smem, vmem = pl.BlockSpec(memory_space=pltpu.SMEM), pl.BlockSpec(memory_space=pltpu.VMEM)
    hbm = pl.BlockSpec(memory_space=pl.ANY)
    buffer = lambda *shape: pltpu.VMEM(shape + (span,), jnp.float32)
    dma = pltpu.SemaphoreType.DMA
    return pl.pallas_call(
        functools.partial(serve_kernel, room),
        in_specs=[smem] * len(tables) + [hbm, vmem],
        out_specs=[hbm, hbm, vmem, vmem],
        out_shape=[
            jax.ShapeDtypeStruct((targets, FULL) + shape, dtype),
            jax.ShapeDtypeStruct((NDP, lanes, span), jnp.float32),
            jax.ShapeDtypeStruct((NDP, 1, span), jnp.float32),
            jax.ShapeDtypeStruct((grains, GRAIN), jnp.float32),
        ],
        scratch_shapes=[
            pltpu.VMEM(shares.shape, dtype),
            pltpu.VMEM((targets, room) + shape, dtype),
            [pltpu.VMEM((targets // 2, room) + shape, dtype)] * 2,
            buffer(NDP, lanes),
            pltpu.VMEM((stored, lanes, 1), jnp.float32),
            buffer(NDP, 2),
            buffer(NDP, 2), buffer(listed, 2), buffer(NQ - 1, listed, 2), buffer(listed, 1), buffer(NDP, 1), buffer(NDP, 1),
            dma((2,)), dma((2, targets // 2)), dma((2, targets // 2)), dma((2, 2, 2)), dma((3, 2)),
        ],
        compiler_params=pltpu.CompilerParams(
            collective_id=collective_id, has_side_effects=True, vmem_limit_bytes=VMEM_LIMIT
        ),
        cost_estimate=pl.CostEstimate(
            flops=2 * NDP * lanes * span * width,
            bytes_accessed=2 * (shares.size + 3 * targets * room * shape[0] * shape[1]),
            transcendentals=NDP * lanes * span,
        ),
    )(*tables, shares, centroids)


def on_device(embeddings, point_parent, parent_list, block_slots, centroids):
    y, z, c, q = (lax.axis_index(a) for a in ("y", "z", "core", "cand"))
    here = (y * NZ + z) * NC + c
    row_count, width = embeddings.shape
    stored = centroids.shape[0]
    listed = parent_list.shape[1]
    grains = row_count // GRAIN
    local = grains // NQ
    i32 = jnp.int32

    share = lax.dynamic_index_in_dim(embeddings.reshape(local, NQ, GRAIN, width), q, 1, keepdims=False)
    shares = lax.all_gather(share, ("z", "core"), axis=0, tiled=True)

    counts = jnp.sum((point_parent[:, None] == parent_list[here][None, :]).astype(i32), axis=0)
    counts = census(counts, 1)
    starts = jnp.cumsum(counts, axis=1) - counts
    begin = starts // GRAIN
    last = (starts + counts - 1) // GRAIN
    low = starts % GRAIN
    high = low + counts
    slots = jnp.take(block_slots, parent_list, axis=0)
    owner = slots // (stored * NQ)
    planes = jnp.arange(NQ, dtype=i32)

    def share_of(begin, last, plane):
        nearest = begin + (plane - begin) % NQ
        return nearest, (nearest <= last).astype(i32) + (nearest + NQ <= last).astype(i32)

    loads = share_of(begin[..., None], last[..., None], planes)[1]
    loads = jnp.broadcast_to(loads[:, :, None, :], (NDP, listed, 2, NQ)).reshape(NY, PER_Y * listed * 2, NQ)
    takers = jnp.swapaxes(owner, 2, 3).reshape(NY, PER_Y * listed * 2, NQ)
    takes = takers[..., None] == jnp.arange(NDP, dtype=i32)
    totals = jnp.einsum(
        "ymqj,ymp->yqjp", takes.astype(jnp.bfloat16), loads.astype(jnp.bfloat16), preferred_element_type=jnp.float32
    )
    size = jnp.sum((jnp.max(totals) > jnp.asarray(ROOMS[:-1], jnp.float32)).astype(i32))

    mine = jnp.take(owner, q, axis=2) == here
    entry = jnp.any(mine, axis=2)
    chosen = lambda value: jnp.sum(jnp.where(entry, value, 0), axis=1)
    served = jnp.any(entry, axis=1)
    serve_low, serve_high, serve_begin = chosen(low), chosen(high), chosen(begin)
    serve_last = jnp.where(served, chosen(last), -1)
    serve_block = jnp.sum(jnp.where(mine, jnp.take(slots, q, axis=2) % stored, 0), axis=(1, 2))
    grouped = served.reshape(NY, PER_Y).astype(i32)
    many = jnp.sum(grouped, axis=1)
    rank = jnp.where(
        grouped > 0, jnp.cumsum(grouped, axis=1) - 1, many[:, None] + jnp.cumsum(1 - grouped, axis=1) - 1
    )
    around = jnp.arange(PER_Y, dtype=i32)
    order = jnp.sum(jnp.where(rank[:, :, None] == around, around[None, :, None], 0), axis=1).reshape(-1)
    serving = (serve_block, serve_low, serve_high, order, many)

    _, landing = share_of(serve_begin[:, None], serve_last[:, None], planes)
    landing = landing.reshape(NY, PER_Y, NQ)
    base = (jnp.cumsum(landing, axis=1) - landing).reshape(NDP, NQ)
    step = jnp.arange(SPAN, dtype=i32)
    grain = serve_begin[:, None] + step
    plane = grain % NQ
    within = jnp.sum(jnp.where(plane[..., None] == planes, base[:, None, :], 0), axis=2) + step // NQ
    real = grain <= serve_last[:, None]
    within = jnp.where(real, within, within[:, :1])
    plane = jnp.where(real, plane, plane[:, :1])
    within = jnp.where(served[:, None], within, 0)

    own = lambda value: lax.dynamic_index_in_dim(value, here, 0, keepdims=False)
    dps = jnp.arange(NDP, dtype=i32)
    depth_order = dps.reshape(NY, NZ, NC).transpose(0, 2, 1).reshape(-1)
    own_owner = own(jnp.take(owner, q, axis=2))
    pick = jnp.sum(
        jnp.where(own_owner[None] == depth_order[:, None, None], jnp.arange(listed, dtype=i32)[None, :, None], 0),
        axis=(1, 2),
    )
    deep = lambda index: by_depth(index // PER_Y, index // NC % NZ, index % NC)

    of_y = lambda value: lax.dynamic_index_in_dim(value.reshape((NY, PER_Y) + value.shape[1:]), y, 0, keepdims=False)
    target = (jnp.arange(NY, dtype=i32) * NZ + z) * NC + c
    hit = jnp.any(of_y(owner)[None] == target[:, None, None, None, None], axis=-1)
    sent = lambda value: jnp.sum(jnp.where(hit, of_y(value)[None, :, :, None], 0), axis=2)
    nearest, sending = share_of(sent(begin), jnp.where(jnp.any(hit, axis=2), sent(last), -1), q)
    place = jnp.cumsum(sending, axis=1) - sending
    places = jnp.arange(FULL, dtype=i32)
    picks = 0
    for slot in range(2):
        here_now = (place[..., None] + slot == places) & (sending[..., None] > slot)
        which = around[:, None] * local + nearest // NQ + slot
        picks = picks + jnp.sum(jnp.where(here_now, which[..., None], 0), axis=1)

    tables = (picks.reshape(-1), (plane * FULL + within).reshape(-1), serve_block)
    tables += (deep(own_owner[:, 0]), deep(own_owner[:, 1]), pick, own(begin), own(low), own(high))
    tables = lax.optimization_barrier(tables)

    def finish(most, collective_id, shares, centroids, *tables):
        rows, logits, norms, log_norms = serve(most, collective_id, grains, shares, centroids, *tables)
        rows = rows.reshape(NY, NQ, FULL, GRAIN, width)
        return update(rows, tables[1], serving, most, centroids, logits, norms), log_norms

    branches = [functools.partial(finish, most, 2 + n) for n, most in enumerate(ROOMS)]
    updated, log_norms = lax.switch(size, branches, shares, centroids, *tables)
    return updated, log_norms.reshape(row_count)


def solution(mesh):
    split = Mesh(mesh.devices.reshape(NY, NZ, NC, NQ), ("y", "z", "core", "cand"))
    dp = ("y", "z", "core")
    every = dp + ("cand",)
    return jax.shard_map(
        on_device,
        mesh=split,
        in_specs=(P(dp, None), P(dp), P(), P(), P(every, None, None)),
        out_specs=(P(every, None, None), P(dp)),
        check_vma=False,
    )
```

time: 241 us -> 216 us (0.90)
  Pallas kernels: 173 us -> 151 us
  waiting for transfers between devices: 10.3 us -> 25 us
  local copies, waits for them, and re-layouts: 26.5 us -> 16 us
  other arithmetic: 11.6 us -> 6.58 us
    pallas_call x4 -> x2, Pallas kernels: 158 us -> 136 us  [the longest x1 126 us: serve(): pl.pallas_call(functools.partial(serve_kernel, room), in_specs=[smem] * l...]
    all_gather x1, waiting for transfers between devices: 10.2 us -> 24.9 us  [on_device(): shares = lax.all_gather(share, ('z', 'core'), axis=0, tiled=True)]
  transfers between devices with their start and end apart: 1 -> 1, of which waited for: 1 -> 1; matrix products, arithmetic and copies ran while one was open for 13% -> 9% of each run, Pallas kernels for 6% -> 7%
where the time goes in v4:
time: 216 us; the launch traced here: 215 us
  Pallas kernels  151 us (70%)
  waiting for transfers between devices  25 us (12%)
  local copies, waits for them, and re-layouts  16 us (7%)
  between operations  15.1 us (7%)
  other arithmetic  6.58 us (3%)
    pallas_call x1, Pallas kernels, serve(): pl.pallas_call(functools.partial(serve_kernel, room), in_specs=[smem] * l...  126 us
    all_gather x1, waiting for transfers between devices, on_device(): shares = lax.all_gather(share, ('z', 'core'), axis=0, tiled=True)  24.9 us
    pallas_call x1, Pallas kernels, census(): pl.pallas_call(census_kernel, in_specs=[vmem], out_specs=vmem, out_shape=...  15.2 us
    pallas_call x1, Pallas kernels, update(): pl.pallas_call(functools.partial(update_kernel, room), in_specs=[smem] *...  9.54 us
    gather x3, local copies, waits for them, and re-layouts, on_device(): slots = jnp.take(block_slots, parent_list, axis=0)  5.84 us
  transfers between devices with their start and end apart: 1, of which 1 were waited for; matrix products, arithmetic and copies ran while one was open for 9% of the time, Pallas kernels for 7%

profile of v4, /device:TPU:1, one launch (start us, length us, event | category | flops | bytes accessed | tf_op | source)
XLA Modules:
  0.0 215.3 jit_solution(1543711489744211322)
XLA Ops:
  7.2 1.5 copy-done
  8.8 0.8 constant_dynamic-slice_fusion
  9.7 0.8 copy.61
  10.5 0.9 dynamic-slice_reduce_fusion
  11.4 0.9 convert_reduce_fusion
  12.3 15.2 %shard_map.77 = s32[64,1,128]{2,1,0:T(1,128)S(1)} custom-call(s32[1,128]{1,0:T(1,128)S(1)} %pad_bitcast_fusion.count_ref), custom_call_target="tpu_custom_call" | custom-call | tf_op jit(solution)/shard_map/pallas_call | solution.py:172
  27.5 0.2 reduce_window_sum.49
  27.8 0.9 copy.64
  28.7 3.6 %gather_fusion = s32[1024,4,2]{1,2,0:T(2,128)S(1)} fusion(s32[256,4,2]{1,2,0:T(2,128)S(1)} %copy.64, s32[1024]{0:T(1024)S(1)} %broadcast_clamp_fusion), kind=kCustom, calls=%fused_computation | custom fusion | bytes 69632 | tf_op jit(solution)/shard_map/jit(_take)/gather | solution.py:397
  32.2 1.2 copy.77
  33.5 0.2 fusion.20
  33.7 0.1 fusion.63
  33.9 0.2 reduce_window_sum.54
  34.1 0.1 fusion.66
  34.2 0.2 reduce_window_sum.55
  34.5 0.1 select_reduce_fusion.5
  34.6 0.1 reshape.448
  34.7 0.1 broadcast_in_dim.217
  34.8 0.2 select_reduce_fusion.6
  35.2 0.1 copy.73
  35.4 0.1 bitcast_subtract_fusion
  35.6 0.1 copy.75
  35.7 0.1 add.485
  35.9 0.1 add.469
  36.1 0.1 broadcast_in_dim.222
  36.2 0.1 le.115
  36.4 0.1 broadcast_in_dim.215
  36.5 1.1 copy.69
  37.9 0.4 compare_reduce_fusion
  38.4 0.6 select_reduce_fusion.2
  39.0 0.1 copy.70
  39.2 0.1 copy.71
  39.3 0.2 select_reduce_fusion.1
  39.5 0.2 select_reduce_fusion
  39.9 0.2 select_reduce_fusion.4
  40.1 0.1 add_select_fusion.1
  40.3 1.0 copy.66
  41.2 0.3 copy.67
  41.6 0.5 add_convert_fusion
  42.1 0.3 broadcast_in_dim.199
  42.4 1.1 fusion.2
  43.6 1.4 fusion.57
  45.6 24.9 %all-gather.3.cloned.1.call-done = bf16[256,1,16,1024]{3,2,1,0:T(8,128)(2,1)} async-done(((bf16[16,1,16,1024]{3,2,1,0:T(8,128)(2,1)}), bf16[256,1,16,1024]{3,2,1,0:T(8,128)(2,1)}) %all-gather.3.cloned.1.call-update) | async-done | bytes 8388624 | tf_op jit(solution)/shard_map/all_gather | solution.py:388
  70.6 136.3 %conditional.1 = (bf16[8,128,1024]{2,1,0:T(8,128)(2,1)}, f32[64,16]{1,0:T(8,128)S(1)}) conditional(s32[]{:T(128)} %clamp.3, (s32[512]{0:T(512)S(1)}, s32[512]{0:T(512)S(1)}, s32[64]{0:T(128)S(1)}, s32[16]{0:T(128)S(1)}, s32[16]{0:T(128)S(1)}, /*index=5*/s32[64]{0:T(128)S(1)}, s32[16]{0:T(128)S(1)}, s32[16]{0:T(128)S(1)}, ...), branch_computations={%region_25.27_spmd, %region_26.28_spmd, %region_27.29_spmd, %regio... | conditional | flops 3221225472 | bytes 75497488 | solution.py:475
  70.6 126.4 %branch_0_fun.2 = (bf16[16,32,16,1024]{3,2,1,0:T(8,128)(2,1)}, f32[64,128,128]{2,1,0:T(8,128)}, f32[64,1,128]{2,1,0:T(1,128)}, f32[64,16]{1,0:T(8,128)S(1)}) custom-call(s32[512]{0:T(512)S(1)} %get-tuple-element.135.pick_ref, s32[512]{0:T(512)S(1)} %get-tuple-element.111.spot_ref, s32[64]{0:T(128)S(1)} %get-tuple-element.130.block_ref, ...), custom_call_target="tpu_custom_call" | custom-call | flops 2147483648 | bytes 35127296 | tf_op jit(solution)/shard_map/cond/branch_0_fun/pallas_call | solution.py:346
  196.9 9.5 %branch_0_fun.3 = bf16[8,128,1024]{2,1,0:T(8,128)(2,1)} custom-call(s32[512]{0:T(512)S(1)} %get-tuple-element.111.spot_ref, s32[64]{0:T(128)S(1)} %get-tuple-element.130.block_ref, s32[64]{0:T(128)S(1)} %get-tuple-element.131.low_ref, s32[64]{0:T(128)S(1)} %get-tuple-element.132.high_ref, s32[64]{0:T(128)S(1)} %get-tuple-element.133.order_ref, ...), custom_call_target="tpu_custom_call" | custom-call | flops 1073741824 | bytes 16777216 | tf_op jit(solution)/shard_map/cond/branch_0_fun/pallas_call | solution.py:103
  206.9 0.7 reshape.449
  207.6 0.9 copy-done.1
  (58 shorter events, 1.8 us)
Async XLA Ops:
  7.2 1.6 copy-start
  7.2 63.4 %all-gather.3.cloned.1.call-start = ((), (), s32[]{:S(2)}) async-start(), calls=%async_computation | async-start | bytes 8912896 | tf_op jit(solution)/shard_map/all_gather | solution.py:388
  40.2 3.3 %copy-start.3 = (f32[3]{0:T(128)S(1)}, f32[3]{0:T(128)}, u32[]{:S(2)}) copy-start(f32[3]{0:T(128)} %constant.301.clone) | copy-start | bytes 40
  40.3 30.3 %copy-start.2 = (bf16[8,128,1024]{2,1,0:T(8,128)(2,1)S(1)}, bf16[8,128,1024]{2,1,0:T(8,128)(2,1)}, u32[]{:S(2)}) copy-start(bf16[8,128,1024]{2,1,0:T(8,128)(2,1)} %param.16) | copy-start | bytes 6291460
  206.9 1.6 copy-start.1
Sparse Core Ops, SparseCore 0:
  10.4 60.1 all-gather.2

commit v5 on v4

--- a/solution.py
+++ b/solution.py
@@ -18,7 +18,8 @@
 PER_Y = NZ * NC
 ABREAST = 4
 FULL = 2 * PER_Y
-ROOMS = (17, 19, 22, FULL)
+ROOMS = (16, 17, 20, FULL)
+SPARE = 5
 STEPS = (
     ((1, 1), (3, 3), (1, 3), (3, 1), (1, 0), (3, 0), (1, 2), (3, 2)),
     ((0, 1), (0, 3), (2, 1), (2, 3), (2, 2), (0, 2), (2, 0)),
@@ -187,11 +188,13 @@
     share_ref, cent_ref, rows_ref, logit_ref, got_ref, log_ref,
     grains_ref, send_ref, held_refs, kept_ref, square_ref, part_ref,
     back_ref, half_ref, quarters_ref, own_ref, fore_ref, land_ref,
-    load_sem, send_sem, recv_sem, out_sem, sems,
+    load_sem, send_sem, recv_sem, hand_sem, out_sem, sems,
 ):
     y, z, c, q = (lax.axis_index(a) for a in ("y", "z", "core", "cand"))
     here = y * NQ + q
     deep = by_depth(y, z, c)
+    spare = min(SPARE, FULL - room)
+    front, back = pl.ds(0, room - spare), pl.ds(room - spare, spare)
     peers = plane_peers(y, z, c)
     mates = [(y, z, c, lax.rem(q + d, NQ)) for d in range(1, NQ)]
 
@@ -211,27 +214,35 @@
     def lands(phase, step):
         return held_refs[phase].at[((NY - step[0]) % NY) // 2 * NQ + q]
 
-    def copy(phase, n, places):
+    def copy(phase, n, places, part):
         step = STEPS[phase][n]
         index, device = target(step)
         return pltpu.make_async_remote_copy(
-            send_ref.at[index, places], lands(phase, step).at[places], send_sem.at[phase, n], recv_sem.at[phase, n],
-            device_id=device, device_id_type=MESH,
+            send_ref.at[index, places], lands(phase, step).at[places],
+            send_sem.at[phase, part, n], recv_sem.at[phase, part, n], device_id=device, device_id_type=MESH,
         )
 
     for phase, steps in enumerate(STEPS):
 
         @pl.loop(0, room)
-        def _(place):
+        def _(turn):
+            place, part = (turn + room - spare) % room, (turn + room - spare) // room
             for n, step in enumerate(steps):
                 index, _ = target(step)
                 send_ref[index, place] = grains_ref[pick_ref[index * FULL + place]]
-                copy(phase, n, pl.ds(place, 1)).start()
+                copy(phase, n, pl.ds(place, 1), part).start()
             if phase == 1:
                 send_ref[here, place] = grains_ref[pick_ref[here * FULL + place]]
 
-    kept = pltpu.make_async_copy(send_ref.at[here], lands(1, (0, 0)), load_sem.at[1])
+    kept = pltpu.make_async_copy(send_ref.at[here], lands(1, (0, 0)).at[pl.ds(0, room)], load_sem.at[1])
     kept.start()
+
+    def hand(phase):
+        held_ref = held_refs[phase]
+        return pltpu.make_async_remote_copy(
+            held_ref.at[:, back], held_ref.at[:, pl.ds(room, spare)], hand_sem.at[phase, 0], hand_sem.at[phase, 1],
+            device_id=(y, z, 1 - c, q), device_id_type=MESH,
+        )
 
     @pl.loop(0, cent_ref.shape[0])
     def _(b):
@@ -244,7 +255,7 @@
     def rows_out(phase, side):
         return pltpu.make_async_copy(
             held_refs[phase].at[pl.ds(side * NQ, NQ)],
-            rows_ref.at[pl.ds(group_of(phase, side) * NQ, NQ), pl.ds(0, room)],
+            rows_ref.at[pl.ds(group_of(phase, side) * NQ, NQ), pl.ds(0, room + spare)],
             out_sem.at[phase, side, 0],
         )
 
@@ -254,10 +265,16 @@
 
     for phase, steps in enumerate(STEPS):
         held_ref = held_refs[phase]
-        for n in range(len(steps)):
-            copy(phase, n, pl.ds(0, room)).wait()
         if phase == 1:
             kept.wait()
+        if spare:
+            for n in range(len(steps)):
+                copy(phase, n, back, 0).wait()
+            hand(phase).start()
+        for n in range(len(steps)):
+            copy(phase, n, front, 1).wait()
+        if spare:
+            hand(phase).wait()
         turns = PER_Y // ABREAST
 
         for side in range(2):
@@ -356,12 +373,12 @@
         scratch_shapes=[
             pltpu.VMEM(shares.shape, dtype),
             pltpu.VMEM((targets, room) + shape, dtype),
-            [pltpu.VMEM((targets // 2, room) + shape, dtype)] * 2,
+            [pltpu.VMEM((targets // 2, room + min(SPARE, FULL - room)) + shape, dtype)] * 2,
             buffer(NDP, lanes),
             pltpu.VMEM((stored, lanes, 1), jnp.float32),
             buffer(NDP, 2),
             buffer(NDP, 2), buffer(listed, 2), buffer(NQ - 1, listed, 2), buffer(listed, 1), buffer(NDP, 1), buffer(NDP, 1),
-            dma((2,)), dma((2, targets // 2)), dma((2, targets // 2)), dma((2, 2, 2)), dma((3, 2)),
+            dma((2,)), dma((2, 2, targets // 2)), dma((2, 2, targets // 2)), dma((2, 2)), dma((2, 2, 2)), dma((3, 2)),
         ],
         compiler_params=pltpu.CompilerParams(
             collective_id=collective_id, has_side_effects=True, vmem_limit_bytes=VMEM_LIMIT
@@ -409,7 +426,10 @@
     totals = jnp.einsum(
         "ymqj,ymp->yqjp", takes.astype(jnp.bfloat16), loads.astype(jnp.bfloat16), preferred_element_type=jnp.float32
     )
-    size = jnp.sum((jnp.max(totals) > jnp.asarray(ROOMS[:-1], jnp.float32)).astype(i32))
+    paired = jnp.sum(totals.reshape(NY, NQ, NDP // NC, NC, NQ), axis=3)
+    rooms = jnp.asarray(ROOMS[:-1], jnp.float32)
+    size = jnp.sum(((jnp.max(paired) > 2 * rooms) | (jnp.max(totals) > rooms + SPARE)).astype(i32))
+    room = jnp.asarray(ROOMS, i32)[size]
 
     mine = jnp.take(owner, q, axis=2) == here
     entry = jnp.any(mine, axis=2)
@@ -437,6 +457,7 @@
     real = grain <= serve_last[:, None]
     within = jnp.where(real, within, within[:, :1])
     plane = jnp.where(real, plane, plane[:, :1])
+    within = jnp.where(within < room, within, 2 * room + SPARE - 1 - within)
     within = jnp.where(served[:, None], within, 0)
 
     own = lambda value: lax.dynamic_index_in_dim(value, here, 0, keepdims=False)
@@ -450,18 +471,20 @@
     deep = lambda index: by_depth(index // PER_Y, index // NC % NZ, index % NC)
 
     of_y = lambda value: lax.dynamic_index_in_dim(value.reshape((NY, PER_Y) + value.shape[1:]), y, 0, keepdims=False)
-    target = (jnp.arange(NY, dtype=i32) * NZ + z) * NC + c
-    hit = jnp.any(of_y(owner)[None] == target[:, None, None, None, None], axis=-1)
-    sent = lambda value: jnp.sum(jnp.where(hit, of_y(value)[None, :, :, None], 0), axis=2)
-    nearest, sending = share_of(sent(begin), jnp.where(jnp.any(hit, axis=2), sent(last), -1), q)
-    place = jnp.cumsum(sending, axis=1) - sending
+    target = (jnp.arange(NY, dtype=i32)[:, None] * NZ + z) * NC + jnp.arange(NC, dtype=i32)
+    hit = jnp.any(of_y(owner) == target[:, :, None, None, None, None], axis=-1)
+    sent = lambda value: jnp.sum(jnp.where(hit, of_y(value)[:, :, None], 0), axis=3)
+    nearest, sending = share_of(sent(begin), jnp.where(jnp.any(hit, axis=3), sent(last), -1), q)
+    place = jnp.cumsum(sending, axis=2) - sending
     places = jnp.arange(FULL, dtype=i32)
+    straight = (jnp.arange(NC, dtype=i32) == c)[None, :, None, None]
     picks = 0
     for slot in range(2):
-        here_now = (place[..., None] + slot == places) & (sending[..., None] > slot)
+        spot = place + slot
+        spot = jnp.where(straight, jnp.where(spot < room, spot, -1), jnp.where(spot < room, -1, 2 * room - 1 - spot))
+        here_now = (spot[..., None] == places) & (sending[..., None] > slot)
         which = around[:, None] * local + nearest // NQ + slot
-        picks = picks + jnp.sum(jnp.where(here_now, which[..., None], 0), axis=1)
-
+        picks = picks + jnp.sum(jnp.where(here_now, which[..., None], 0), axis=(1, 2))
     tables = (picks.reshape(-1), (plane * FULL + within).reshape(-1), serve_block)
     tables += (deep(own_owner[:, 0]), deep(own_owner[:, 1]), pick, own(begin), own(low), own(high))
     tables = lax.optimization_barrier(tables)
@@ -469,7 +492,8 @@
     def finish(most, collective_id, shares, centroids, *tables):
         rows, logits, norms, log_norms = serve(most, collective_id, grains, shares, centroids, *tables)
         rows = rows.reshape(NY, NQ, FULL, GRAIN, width)
-        return update(rows, tables[1], serving, most, centroids, logits, norms), log_norms
+        used = min(most + SPARE, FULL)
+        return update(rows, tables[1], serving, used, centroids, logits, norms), log_norms
 
     branches = [functools.partial(finish, most, 2 + n) for n, most in enumerate(ROOMS)]
     updated, log_norms = lax.switch(size, branches, shares, centroids, *tables)

time: 216 us -> 212 us (0.981)
  waiting for transfers between devices: 25 us -> 17.2 us
  other arithmetic: 6.58 us -> 11.3 us
  Pallas kernels: 151 us -> 148 us
  between operations: 15.1 us -> 17.4 us
    all_gather x1, waiting for transfers between devices: 24.9 us -> 17.2 us  [on_device(): shares = lax.all_gather(share, ('z', 'core'), axis=0, tiled=True)]
    pallas_call x1, Pallas kernels: 126 us -> 122 us  [serve(): pl.pallas_call(functools.partial(serve_kernel, room), in_specs=[smem] * l...]
    reduce_sum x4 -> x5, other arithmetic: 2.36 us -> 4.36 us  [the longest x1 1.96 us: on_device(): jnp.sum(((jnp.max(paired) > 2 * rooms) | (jnp.max(totals) > rooms + SPARE...]
  transfers between devices with their start and end apart: 1 -> 1, of which waited for: 1 -> 1; matrix products, arithmetic and copies ran while one was open for 9% -> 12% of each run, Pallas kernels for 7% -> 7%
where the time goes in v5:
time: 212 us
  Pallas kernels  148 us (70%)
  between operations  17.4 us (8%)
  waiting for transfers between devices  17.2 us (8%)
  local copies, waits for them, and re-layouts  16.8 us (8%)
  other arithmetic  11.3 us (5%)
    pallas_call x1, Pallas kernels, serve(): pl.pallas_call(functools.partial(serve_kernel, room), in_specs=[smem] * l...  122 us
    all_gather x1, waiting for transfers between devices, on_device(): shares = lax.all_gather(share, ('z', 'core'), axis=0, tiled=True)  17.2 us
    pallas_call x1, Pallas kernels, census(): pl.pallas_call(census_kernel, in_specs=[vmem], out_specs=vmem, out_shape=...  15.2 us
    pallas_call x1, Pallas kernels, update(): pl.pallas_call(functools.partial(update_kernel, room), in_specs=[smem] *...  10.8 us
    gather x3, local copies, waits for them, and re-layouts, on_device(): slots = jnp.take(block_slots, parent_list, axis=0)  5.84 us
  transfers between devices with their start and end apart: 1, of which 1 were waited for; matrix products, arithmetic and copies ran while one was open for 12% of the time, Pallas kernels for 7%

profile of v5, /device:TPU:1, one launch (start us, length us, event | category | flops | bytes accessed | tf_op | source)
XLA Modules:
  0.0 212.3 jit_solution(14540614388338952998)
XLA Ops:
  7.2 1.5 copy-done
  8.8 0.8 constant_dynamic-slice_fusion
  9.6 0.8 copy.89
  10.4 0.9 dynamic-slice_reduce_fusion
  11.3 0.9 convert_reduce_fusion
  12.2 15.2 %shard_map.86 = s32[64,1,128]{2,1,0:T(1,128)S(1)} custom-call(s32[1,128]{1,0:T(1,128)S(1)} %pad_bitcast_fusion.count_ref), custom_call_target="tpu_custom_call" | custom-call | tf_op jit(solution)/shard_map/pallas_call | solution.py:173
  27.4 0.2 reduce_window_sum.54
  27.7 0.9 copy.92
  28.6 3.6 %gather_fusion = s32[1024,4,2]{1,2,0:T(2,128)S(1)} fusion(s32[256,4,2]{1,2,0:T(2,128)S(1)} %copy.92, s32[1024]{0:T(1024)S(1)} %broadcast_clamp_fusion), kind=kCustom, calls=%fused_computation | custom fusion | bytes 69632 | tf_op jit(solution)/shard_map/jit(_take)/gather | solution.py:414
  32.1 1.2 copy.106
  33.4 0.1 add_select_fusion.1
  33.5 1.0 copy.94
  34.5 0.3 copy.95
  34.9 0.2 fusion.19
  35.1 0.1 fusion.68
  35.2 0.2 select_reduce_fusion.6
  35.4 0.5 add_convert_fusion
  35.9 0.3 broadcast_in_dim.218
  36.2 1.1 fusion.72
  37.4 0.2 copy.97
  37.6 0.6 reduce_sum.145
  38.3 0.7 reduce_max.18
  39.0 2.0 fusion.58
  42.9 0.2 reduce_window_sum.59
  43.0 0.1 fusion.71
  43.2 0.2 reduce_window_sum.60
  43.4 0.1 select_reduce_fusion.5
  43.7 0.1 broadcast_in_dim.237
  44.8 0.1 broadcast_in_dim.242
  45.0 0.1 le.115
  45.2 0.1 broadcast_in_dim.235
  45.3 1.1 copy.99
  46.8 0.7 compare_reduce_fusion
  47.5 1.2 select_reduce_fusion.2
  48.7 0.1 copy.100
  48.9 0.1 copy.101
  49.6 0.7 dynamic_slice.39
  51.1 0.8 fusion.38
  51.8 0.3 select_reduce_fusion.1
  52.1 0.3 select_reduce_fusion
  52.5 0.2 select_reduce_fusion.4
  52.7 0.7 fusion.56
  53.4 17.2 %all-gather.3.cloned.1.call-done = bf16[256,1,16,1024]{3,2,1,0:T(8,128)(2,1)} async-done(((bf16[16,1,16,1024]{3,2,1,0:T(8,128)(2,1)}), bf16[256,1,16,1024]{3,2,1,0:T(8,128)(2,1)}) %all-gather.3.cloned.1.call-update) | async-done | bytes 8388624 | tf_op jit(solution)/shard_map/all_gather | solution.py:405
  70.6 133.2 %conditional.1 = (bf16[8,128,1024]{2,1,0:T(8,128)(2,1)}, f32[64,16]{1,0:T(8,128)S(1)}) conditional(s32[]{:T(128)} %clamp.3, (s32[512]{0:T(512)S(1)}, s32[512]{0:T(512)S(1)}, s32[64]{0:T(128)S(1)}, s32[16]{0:T(128)S(1)}, s32[16]{0:T(128)S(1)}, /*index=5*/s32[64]{0:T(128)S(1)}, s32[16]{0:T(128)S(1)}, s32[16]{0:T(128)S(1)}, ...), branch_computations={%region_27.29_spmd, %region_28.30_spmd, %region_29.31_spmd, %regio... | conditional | flops 3221225472 | bytes 83886128 | solution.py:499
  70.6 122.2 %branch_0_fun.2 = (bf16[16,32,16,1024]{3,2,1,0:T(8,128)(2,1)}, f32[64,128,128]{2,1,0:T(8,128)}, f32[64,1,128]{2,1,0:T(1,128)}, f32[64,16]{1,0:T(8,128)S(1)}) custom-call(s32[512]{0:T(512)S(1)} %get-tuple-element.135.pick_ref, s32[512]{0:T(512)S(1)} %get-tuple-element.111.spot_ref, s32[64]{0:T(128)S(1)} %get-tuple-element.130.block_ref, ...), custom_call_target="tpu_custom_call" | custom-call | flops 2147483648 | bytes 33554432 | tf_op jit(solution)/shard_map/cond/branch_0_fun/pallas_call | solution.py:363
  192.8 10.8 %branch_0_fun.3 = bf16[8,128,1024]{2,1,0:T(8,128)(2,1)} custom-call(s32[512]{0:T(512)S(1)} %get-tuple-element.111.spot_ref, s32[64]{0:T(128)S(1)} %get-tuple-element.130.block_ref, s32[64]{0:T(128)S(1)} %get-tuple-element.131.low_ref, s32[64]{0:T(128)S(1)} %get-tuple-element.132.high_ref, s32[64]{0:T(128)S(1)} %get-tuple-element.133.order_ref, ...), custom_call_target="tpu_custom_call" | custom-call | flops 1073741824 | bytes 16777216 | tf_op jit(solution)/shard_map/cond/branch_0_fun/pallas_call | solution.py:104
  203.9 0.7 reshape.492
  204.5 0.9 copy-done.1
  (67 shorter events, 2.4 us)
Async XLA Ops:
  7.2 1.6 copy-start
  7.2 63.5 %all-gather.3.cloned.1.call-start = ((), (), s32[]{:S(2)}) async-start(), calls=%async_computation | async-start | bytes 8912896 | tf_op jit(solution)/shard_map/all_gather | solution.py:405
  35.1 4.0 %copy-start.6 = (f32[3]{0:T(128)S(1)}, f32[3]{0:T(128)}, u32[]{:S(2)}) copy-start(f32[3]{0:T(128)} %constant.341) | copy-start | bytes 40
  35.1 4.0 %copy-start.7 = (f32[3]{0:T(128)S(1)}, f32[3]{0:T(128)}, u32[]{:S(2)}) copy-start(f32[3]{0:T(128)} %constant.340) | copy-start | bytes 40
  44.0 5.6 %copy-start.8 = (s32[4]{0:T(128)S(1)}, s32[4]{0:T(128)}, u32[]{:S(2)}) copy-start(s32[4]{0:T(128)} %constant.317.clone) | copy-start | bytes 52
  70.6 122.2 %copy-start.2 = (bf16[8,128,1024]{2,1,0:T(8,128)(2,1)S(1)}, bf16[8,128,1024]{2,1,0:T(8,128)(2,1)}, u32[]{:S(2)}) copy-start(bf16[8,128,1024]{2,1,0:T(8,128)(2,1)} %get-tuple-element.144.cent_ref) | copy-start | bytes 6291460 | tf_op jit(solution)/shard_map/cond
  203.9 1.6 copy-start.1
Sparse Core Ops, SparseCore 0:
  10.4 60.1 all-gather.2
